TPU v7x, 32 devices: a whole 2x2x4 slice. The times are simulated.
32 devices in a mesh: groups: 1, tok: 32 (over z, y, x, core).
Axes of the slice: x: 2, y: 2, z: 4, core: 2. Of those that a mesh axis runs over, the one named last changes fastest.
Arguments:
- clean_keys: bfloat16 [8192, 2048], P(('groups', 'tok')), may hold values from -12.5 to 12.5
- clean_values: bfloat16 [8192, 2048], P(('groups', 'tok')), may hold values from -12 to 12
- clean_rates: float32 [8192, 4], P(('groups', 'tok')), may hold values from 0.2 to 3.75
- w_in: bfloat16 [4, 512, 512], replicated, may hold values from -0.25 to 0.25
- w_gate: bfloat16 [4, 512, 512], replicated, may hold values from -0.25 to 0.25
- w_out: bfloat16 [4, 512, 512], replicated, may hold values from -0.25 to 0.25
- noisy_tokens: bfloat16 [8192, 2048], P(('groups', 'tok')), may hold values from -5 to 5
- swa_keys: bfloat16 [8192, 2048], P(('groups', 'tok')), may hold values from -250 to 250
- swa_values: bfloat16 [8192, 2048], P(('groups', 'tok')), may hold values from -30 to 30
- level_ids: int32 [64], P(('groups', 'tok')), may hold values from 0 to 7
- window_reach: int32 [64], P(('groups', 'tok')), may hold values from 2 to 1024, as said below
- level_mod: float32 [8, 4096], replicated, may hold values from -3 to 3
- mem_gain: float32 [2048], replicated, may hold values from 0.1 to 1.9
Outputs:
- layer_out: bfloat16 [8192, 2048], P(('groups', 'tok'))
Inputs may be any that keep to these rules, and one draw needn't show every extreme that they name: `window_reach`: number of latest positions, the token's own included, that each block of noisy tokens attends to; some block has 1024.
All inputs are finite; a program needn't handle non-finite values.
Results may differ from a plain program's by a relative error of at most 0.0063.
The roundings to bfloat16 on the way count: a program that leaves them out, or rounds other values in their place, can miss the bound.
Values may be sent and summed in bfloat16 or wider, within the bound.
A program may use at most 128 MiB of HBM per device.

v0:
```python
import jax
import jax.numpy as jnp
from jax import lax
from jax.sharding import PartitionSpec as P

SWDH = 128
WIN = 1024
BLOCK = 128
NLEVEL = 8


epsilon = 1e-06
update_step = 0.05


def shifted(block, axis, distance):
    devices = range(lax.axis_size(axis))
    route = [(i - distance, i) for i in devices if i - distance in devices]
    return lax.ppermute(block, axis, route)


def renormalize(row_share, row_start, initial, grad_scale):
    base_rows = lax.dynamic_slice_in_dim(initial, row_start, row_share.shape[0], 0).astype(
        jnp.float32
    )
    update = base_rows + update_step * row_share * grad_scale
    target = jnp.sqrt(jnp.mean(base_rows * base_rows, axis=-1, keepdims=True))
    return (
        update * target * lax.rsqrt(jnp.mean(update * update, axis=-1, keepdims=True) + epsilon)
    ).astype(jnp.bfloat16)


def local(
    clean_keys,
    clean_values,
    clean_rates,
    w_in,
    w_gate,
    w_out,
    noisy_tokens,
    swa_keys,
    swa_values,
    level_ids,
    window_reach,
    level_mod,
    mem_gain,
):
    row_count = clean_keys.shape[0]
    head_count = w_in.shape[0]
    head_size = w_in.shape[1]
    flat_width = head_count * head_size
    position = lax.axis_index("tok")
    key_heads = clean_keys.reshape(row_count, head_count, head_size)
    value_heads = clean_values.reshape(row_count, head_count, head_size)
    first_proj = jnp.einsum("thd,hfd->thf", key_heads, w_in, preferred_element_type=jnp.float32)
    second = jnp.einsum("thd,hfd->thf", key_heads, w_gate, preferred_element_type=jnp.float32)
    sigmoid = jax.nn.sigmoid(first_proj)
    active = first_proj * sigmoid
    hidden = (active * second).astype(jnp.bfloat16)
    scaled = (clean_rates[:, :, None] * value_heads.astype(jnp.float32)).astype(jnp.bfloat16)
    g_out = jnp.einsum("thd,thf->hdf", scaled, hidden, preferred_element_type=jnp.float32).reshape(
        flat_width, head_size
    )
    d_act = jnp.einsum("thd,hdf->thf", scaled, w_out, preferred_element_type=jnp.float32)
    d_first = (d_act * second * sigmoid * (1.0 + first_proj * (1.0 - sigmoid))).astype(jnp.bfloat16)
    d_second = (d_act * active).astype(jnp.bfloat16)
    g_in = jnp.einsum(
        "thf,thd->hfd", d_first, key_heads, preferred_element_type=jnp.float32
    ).reshape(flat_width, head_size)
    g_gate = jnp.einsum(
        "thf,thd->hfd", d_second, key_heads, preferred_element_type=jnp.float32
    ).reshape(flat_width, head_size)
    initial = jnp.concatenate(
        [
            w_in.reshape(flat_width, head_size),
            w_gate.reshape(flat_width, head_size),
            w_out.reshape(flat_width, head_size),
        ],
        axis=0,
    )
    row_share = lax.psum_scatter(
        jnp.concatenate([g_in, g_gate, g_out], axis=0), "tok", scatter_dimension=0, tiled=True
    )
    power_sum = jnp.sum(row_share * row_share)
    total_power = lax.psum(power_sum, "tok")
    grad_scale = lax.rsqrt(total_power / (3 * flat_width * head_size) + epsilon)
    new_rows = renormalize(row_share, position * row_share.shape[0], initial, grad_scale)
    memories = lax.all_gather(new_rows, "tok", axis=0, tiled=True)
    in_all = memories[: 2 * flat_width]
    out_all = memories[2 * flat_width :]
    mem_in = in_all[:flat_width].reshape(head_count, head_size, head_size)
    mem_gate = in_all[flat_width:].reshape(head_count, head_size, head_size)
    mem_out = out_all.reshape(head_count, head_size, head_size)
    frame_count = level_ids.shape[0]
    chosen = (level_ids[:, None] == jnp.arange(NLEVEL, dtype=jnp.int32)[None, :]).astype(
        jnp.float32
    )
    modulation = jnp.dot(
        chosen, level_mod, preferred_element_type=jnp.float32, precision=lax.Precision.HIGHEST
    )
    modulation = jnp.broadcast_to(
        modulation[:, None, :], (frame_count, BLOCK, 2 * flat_width)
    ).reshape(row_count, 2 * flat_width)
    noisy_rows = noisy_tokens.astype(jnp.float32)
    inverse = lax.rsqrt(jnp.mean(noisy_rows * noisy_rows, axis=-1, keepdims=True) + epsilon)
    queries = (
        noisy_rows * inverse * (1.0 + modulation[:, :flat_width]) + modulation[:, flat_width:]
    ).astype(jnp.bfloat16)
    query_heads = queries.reshape(row_count, head_count, head_size)
    first_apply = jnp.einsum(
        "thd,hfd->thf", query_heads, mem_in, preferred_element_type=jnp.float32
    )
    second_apply = jnp.einsum(
        "thd,hfd->thf", query_heads, mem_gate, preferred_element_type=jnp.float32
    )
    mixture = (jax.nn.silu(first_apply) * second_apply).astype(jnp.bfloat16)
    recalled = jnp.einsum("thf,hdf->thd", mixture, mem_out, preferred_element_type=jnp.float32)
    recalled = (
        recalled
        * lax.rsqrt(jnp.mean(recalled * recalled, axis=-1, keepdims=True) + epsilon)
        * mem_gain.reshape(head_count, head_size)
    )
    reach_shards = WIN // row_count
    earlier = []
    carried = (swa_keys, swa_values)
    for hop_index in range(reach_shards):
        carried = shifted((carried[0], carried[1]), "tok", 1)
        earlier.insert(0, carried)
    key_window = jnp.concatenate([pair[0] for pair in earlier] + [swa_keys], axis=0)
    value_window = jnp.concatenate([pair[1] for pair in earlier] + [swa_values], axis=0)
    key_span = key_window.shape[0]
    sw_heads = flat_width // SWDH
    query_pos = position * row_count + jnp.arange(row_count, dtype=jnp.int32)
    key_pos = (position - reach_shards) * row_count + jnp.arange(key_span, dtype=jnp.int32)
    reach_rows = jnp.broadcast_to(window_reach[:, None], (frame_count, BLOCK)).reshape(row_count)
    visible = (
        (key_pos[None, :] <= query_pos[:, None])
        & (key_pos[None, :] > query_pos[:, None] - reach_rows[:, None])
        & (key_pos[None, :] >= 0)
    )
    scores = jnp.einsum(
        "qsd,ksd->sqk",
        noisy_tokens.reshape(row_count, sw_heads, SWDH),
        key_window.reshape(key_span, sw_heads, SWDH),
        preferred_element_type=jnp.float32,
    ) * SWDH ** (-0.5)
    scores = jnp.where(visible[None, :, :], scores, -1e30)
    row_max = jnp.max(scores, axis=-1, keepdims=True)
    weights = jnp.exp(scores - row_max)
    totals = jnp.sum(weights, axis=-1)
    attended = jnp.einsum(
        "sqk,ksd->qsd",
        weights.astype(jnp.bfloat16),
        value_window.reshape(key_span, sw_heads, SWDH),
        preferred_element_type=jnp.float32,
    )
    attended = attended / jnp.transpose(totals)[:, :, None]
    return (
        recalled.reshape(row_count, flat_width) + attended.reshape(row_count, flat_width)
    ).astype(jnp.bfloat16)


def solution(mesh):
    return jax.shard_map(
        local,
        mesh=mesh,
        in_specs=(
            P(("groups", "tok"), None),
            P(("groups", "tok"), None),
            P(("groups", "tok"), None),
            P(),
            P(),
            P(),
            P(("groups", "tok"), None),
            P(("groups", "tok"), None),
            P(("groups", "tok"), None),
            P(("groups", "tok")),
            P(("groups", "tok")),
            P(),
            P(),
        ),
        out_specs=P(("groups", "tok"), None),
        check_vma=False,
    )
```

profile of v0, /device:TPU:8, one launch (start us, length us, event | category | flops | bytes accessed | tf_op | source)
XLA Modules:
  0.0 422.0 jit_solution(12271460324586918921)
XLA Ops:
  6.5 2.7 copy.60
  10.1 0.8 copy-done.4
  13.9 0.9 fusion.29
  14.7 1.0 fusion.27
  15.7 1.2 fusion.34
  16.9 5.5 %pad_maximum_fusion = f32[6144,512]{1,0:T(8,128)} fusion(f32[2048,512]{1,0:T(8,128)S(1)} %bitcast.148, f32[2048,512]{1,0:T(8,128)S(1)} %bitcast.149, f32[2048,512]{1,0:T(8,128)S(1)} %bitcast.150), kind=kLoop, calls=%fused_computation.4 | loop fusion | flops 6291456 | bytes 25165824 | tf_op jit(solution)/shard_map/concatenate | solution.py:82
  22.5 156.6 %reduce-scatter.2.cloned.1.call-done = f32[192,512]{1,0:T(8,128)} async-done(((f32[6144,512]{1,0:T(8,128)}), f32[192,512]{1,0:T(8,128)}) %reduce-scatter.2.cloned.1.call-update) | async-done | bytes 393232 | tf_op jit(solution)/shard_map/reduce_scatter | solution.py:81
  179.1 1.7 multiply_reduce_fusion.1
  180.8 39.3 %psum.7 = f32[]{:T(128)} all-reduce(f32[]{:T(128)} %multiply_reduce_fusion.1), channel_id=1, replica_groups=mesh['groups'=1,'tok'=32] {'tok'}, use_global_device_ids=true, to_apply=%region_2.0 | all-reduce | flops 1 | bytes 8 | tf_op jit(solution)/shard_map/psum | solution.py:85
  220.8 1.4 fusion.47
  223.1 1.9 collective-permute-start
  225.6 4.3 %collective-permute-start.4 = (bf16[256,2048]{0,1:T(8,128)(2,1)S(1)}, bf16[256,2048]{0,1:T(8,128)(2,1)S(1)}, u32[]{:S(2)}, u32[]{:S(2)}) collective-permute-start(bf16[256,2048]{0,1:T(8,128)(2,1)S(1)} %copy.44), channel_id=1, source_target_pairs={{0,1},{1,2},{2,3},{3,4},{4,5},{5,6},{6,7},{7,8},{8,9},{9,10},{10,1... | collective-permute-start | bytes 3145736 | tf_op jit(solution)/shard_map/ppermute | solution.py:19
  229.8 15.4 %collective-permute-done = bf16[256,2048]{1,0:T(8,128)(2,1)} collective-permute-done((bf16[256,2048]{1,0:T(8,128)(2,1)}, bf16[256,2048]{1,0:T(8,128)(2,1)}, u32[]{:S(2)}, u32[]{:S(2)}) %collective-permute-start) | collective-permute-done | bytes 1048608 | tf_op jit(solution)/shard_map/ppermute | solution.py:19
  245.3 1.9 collective-permute-start.1
  247.2 14.8 %collective-permute-done.4 = bf16[256,2048]{0,1:T(8,128)(2,1)S(1)} collective-permute-done((bf16[256,2048]{0,1:T(8,128)(2,1)S(1)}, bf16[256,2048]{0,1:T(8,128)(2,1)S(1)}, u32[]{:S(2)}, u32[]{:S(2)}) %collective-permute-start.4) | collective-permute-done | bytes 1048608 | tf_op jit(solution)/shard_map/ppermute | solution.py:19
  262.0 1.9 collective-permute-start.5
  263.9 15.1 %collective-permute-done.1 = bf16[256,2048]{1,0:T(8,128)(2,1)S(1)} collective-permute-done((bf16[256,2048]{1,0:T(8,128)(2,1)}, bf16[256,2048]{1,0:T(8,128)(2,1)S(1)}, u32[]{:S(2)}, u32[]{:S(2)}) %collective-permute-start.1) | collective-permute-done | bytes 1048608 | tf_op jit(solution)/shard_map/ppermute | solution.py:19
  279.0 1.9 collective-permute-start.2
  281.5 23.0 %collective-permute-done.5 = bf16[256,2048]{0,1:T(8,128)(2,1)} collective-permute-done((bf16[256,2048]{0,1:T(8,128)(2,1)S(1)}, bf16[256,2048]{0,1:T(8,128)(2,1)}, u32[]{:S(2)}, u32[]{:S(2)}) %collective-permute-start.5) | collective-permute-done | bytes 1048608 | tf_op jit(solution)/shard_map/ppermute | solution.py:19
  304.5 1.9 collective-permute-start.6
  306.4 9.3 %collective-permute-done.2 = bf16[256,2048]{1,0:T(8,128)(2,1)} collective-permute-done((bf16[256,2048]{1,0:T(8,128)(2,1)S(1)}, bf16[256,2048]{1,0:T(8,128)(2,1)}, u32[]{:S(2)}, u32[]{:S(2)}) %collective-permute-start.2) | collective-permute-done | bytes 1048608 | tf_op jit(solution)/shard_map/ppermute | solution.py:19
  315.8 1.9 collective-permute-start.3
  318.2 1.7 fusion.8
  319.8 1.5 copy.61
  321.5 1.6 and_and_fusion
  323.0 4.0 collective-permute-done.6
  327.0 2.1 collective-permute-start.7
  329.1 9.1 %collective-permute-done.3 = bf16[256,2048]{1,0:T(8,128)(2,1)} collective-permute-done((bf16[256,2048]{1,0:T(8,128)(2,1)}, bf16[256,2048]{1,0:T(8,128)(2,1)}, u32[]{:S(2)}, u32[]{:S(2)}) %collective-permute-start.3) | collective-permute-done | bytes 1048608 | tf_op jit(solution)/shard_map/ppermute | solution.py:19
  338.2 2.3 constant_dynamic-update-slice_fusion.4
  340.6 2.3 constant_dynamic-update-slice_fusion.3
  342.9 1.0 constant_dynamic-update-slice_fusion.2
  343.9 2.3 constant_dynamic-update-slice_fusion.1
  346.3 1.0 constant_dynamic-update-slice_fusion
  347.3 7.9 %copy.43 = bf16[1280,2048]{0,1:T(8,128)(2,1)} copy(bf16[1280,2048]{1,0:T(8,128)(2,1)} %constant_dynamic-update-slice_fusion) | data formatting | bytes 10485760 | tf_op jit(solution)/shard_map/concatenate | solution.py:130
  355.2 2.4 constant_dynamic-update-slice_fusion.9
  357.6 2.4 constant_dynamic-update-slice_fusion.8
  360.0 2.3 constant_dynamic-update-slice_fusion.7
  362.4 1.1 constant_dynamic-update-slice_fusion.6
  363.4 1.1 constant_dynamic-update-slice_fusion.5
  364.5 12.8 %fusion.60 = (f32[16,256]{1,0:T(8,128)S(1)}, f32[16,256,1280]{1,2,0:T(8,128)}) fusion(bf16[1280,16,128]{0,2,1:T(8,128)(2,1)} %bitcast.20, pred[256,1280]{0,1:T(8,128)(4,1)S(1)} %copy-done.9, bf16[256,2048]{1,0:T(8,128)(2,1)S(1)} %copy-done.2), kind=kOutput, calls=%fused_computation.100 | convolution fusion | flops 1357901824 | bytes 27607040 | tf_op jit(solution)/shard_map/qsd,ksd->sqk/dot_general | solution.py:141
  377.3 8.7 %fusion = f32[16,256]{1,0:T(8,128)S(1)} fusion(f32[16,256,1280]{1,2,0:T(8,128)} %get-tuple-element.14, f32[16,256]{1,0:T(8,128)S(1)} %get-tuple-element.13), kind=kLoop, calls=%fused_computation.2 | loop fusion | flops 10481664 | bytes 21004288 | tf_op jit(solution)/shard_map/reduce_sum | solution.py:150
  386.0 9.0 %bitcast_divide_fusion = f32[256,16,128]{0,2,1:T(8,128)S(1)} fusion(bf16[1280,16,128]{0,2,1:T(8,128)(2,1)S(1)} %bitcast.132, f32[16,256,1280]{1,2,0:T(8,128)} %get-tuple-element.14, f32[16,256]{1,0:T(8,128)S(1)} %get-tuple-element.13, f32[256,16]{0,1:T(8,128)S(1)} %bitcast.153), kind=kOutput, calls=%fused_computation.17 | convolution fusion | flops 1353187328 | bytes 28344320 | tf_op jit(solution)/shard_map/sqk,ksd->qsd/dot_general | solution.py:151
  395.0 1.8 copy.50
  396.8 5.3 %fusion.59 = (bf16[2048,512]{1,0:T(8,128)(2,1)}, bf16[2048,512]{1,0:T(8,128)(2,1)S(1)}, bf16[2048,512]{1,0:T(8,128)(2,1)}) fusion(bf16[6144,512]{1,0:T(8,128)(2,1)} %all-gather.2.cloned.1.call-done), kind=kLoop, calls=%fused_computation.99 | loop fusion | bytes 12582912 | tf_op jit(solution)/shard_map/slice | solution.py:92
  402.9 5.0 %fusion.9 = (f32[256,4]{0,1:T(4,128)S(1)}, f32[4,512,256]{2,1,0:T(8,128)}) fusion(bf16[4,512,512]{2,1,0:T(8,128)(2,1)} %bitcast.152, f32[4,512,256]{1,2,0:T(8,128)S(1)} %fusion.61, bf16[4,512,512]{2,1,0:T(8,128)(2,1)} %bitcast.151, bf16[256,4,512]{0,2,1:T(8,128)(2,1)S(1)} %bitcast.147), kind=kOutput, calls=%fused_computation.20 | convolution fusion | flops 1077935104 | bytes 9441280 | tf_op jit(solution)/shard_map/thf,hdf->thd/dot_general | solution.py:117
  407.9 1.9 fusion.10
  409.9 1.9 copy.49
  411.7 3.5 add_convert_fusion
  (66 shorter events, 7.1 us)
Async XLA Ops:
  6.5 274.7 %copy-start = (f32[8,4096]{1,0:T(8,128)S(1)}, f32[8,4096]{1,0:T(8,128)}, u32[]{:S(2)}) copy-start(f32[8,4096]{1,0:T(8,128)} %param.24) | copy-start | bytes 393220
  6.5 2.8 copy-start.3
  6.5 2.8 copy-start.7
  6.5 172.5 %reduce-scatter.2.cloned.1.call-start = ((), (), s32[]{:S(2)}) async-start(), calls=%async_computation.1 | async-start | bytes 12976128 | tf_op jit(solution)/shard_map/reduce_scatter | solution.py:81
  9.3 1.6 copy-start.4
  10.9 1.6 copy-start.5
  10.9 2.2 copy-start.6
  10.9 2.2 copy-start.17
  22.5 374.4 %all-gather.2.cloned.1.call-start = ((), (), s32[]{:S(2)}) async-start(), calls=%async_computation.2 | async-start | bytes 6488064 | tf_op jit(solution)/shard_map/all_gather | solution.py:88
  220.7 1.5 copy-start.8
  220.8 4.3 %copy-start.10 = (bf16[256,2048]{1,0:T(8,128)(2,1)S(1)}, bf16[256,2048]{1,0:T(8,128)(2,1)}, u32[]{:S(2)}) copy-start(bf16[256,2048]{1,0:T(8,128)(2,1)} %param.20) | copy-start | bytes 3145732
  222.2 58.7 %copy-start.2 = (bf16[256,2048]{1,0:T(8,128)(2,1)S(1)}, bf16[256,2048]{1,0:T(8,128)(2,1)}, u32[]{:S(2)}) copy-start(bf16[256,2048]{1,0:T(8,128)(2,1)} %param.19) | copy-start | bytes 3145732
  222.2 59.1 %copy-start.18 = (s32[2]{0:T(128)S(1)}, s32[2]{0:T(128)}, u32[]{:S(2)}) copy-start(s32[2]{0:T(128)} %param.22) | copy-start | bytes 28
  223.1 22.2 %collective-permute-start = (bf16[256,2048]{1,0:T(8,128)(2,1)}, bf16[256,2048]{1,0:T(8,128)(2,1)}, u32[]{:S(2)}, u32[]{:S(2)}) collective-permute-start(bf16[256,2048]{1,0:T(8,128)(2,1)} %param.21), channel_id=1, source_target_pairs={{0,1},{1,2},{2,3},{3,4},{4,5},{5,6},{6,7},{7,8},{8,9},{9,10},{10,1... | collective-permute-start | bytes 3145736 | tf_op jit(solution)/shard_map/ppermute | solution.py:19
  225.6 36.5 %collective-permute-start.4 = (bf16[256,2048]{0,1:T(8,128)(2,1)S(1)}, bf16[256,2048]{0,1:T(8,128)(2,1)S(1)}, u32[]{:S(2)}, u32[]{:S(2)}) collective-permute-start(bf16[256,2048]{0,1:T(8,128)(2,1)S(1)} %copy.44), channel_id=1, source_target_pairs={{0,1},{1,2},{2,3},{3,4},{4,5},{5,6},{6,7},{7,8},{8,9},{9,10},{10,1... | collective-permute-start | bytes 3145736 | tf_op jit(solution)/shard_map/ppermute | solution.py:19
  245.3 33.8 %collective-permute-start.1 = (bf16[256,2048]{1,0:T(8,128)(2,1)}, bf16[256,2048]{1,0:T(8,128)(2,1)S(1)}, u32[]{:S(2)}, u32[]{:S(2)}) collective-permute-start(bf16[256,2048]{1,0:T(8,128)(2,1)} %collective-permute-done), channel_id=1, source_target_pairs={{0,1},{1,2},{2,3},{3,4},{4,5},{5,6},{6,7},{7,8},{8,9},{9,10},{10,1... | collective-permute-start | bytes 3145736 | tf_op jit(solution)/shard_map/ppermute | solution.py:19
  262.0 53.7 %copy-start.12 = (bf16[256,2048]{0,1:T(8,128)(2,1)}, bf16[256,2048]{0,1:T(8,128)(2,1)S(1)}, u32[]{:S(2)}) copy-start(bf16[256,2048]{0,1:T(8,128)(2,1)S(1)} %collective-permute-done.4) | copy-start | bytes 3145732
  262.0 42.5 %collective-permute-start.5 = (bf16[256,2048]{0,1:T(8,128)(2,1)S(1)}, bf16[256,2048]{0,1:T(8,128)(2,1)}, u32[]{:S(2)}, u32[]{:S(2)}) collective-permute-start(bf16[256,2048]{0,1:T(8,128)(2,1)S(1)} %collective-permute-done.4), channel_id=1, source_target_pairs={{0,1},{1,2},{2,3},{3,4},{4,5},{5,6},{6,7},{7,8},{8,9},{9,10},{10,1... | collective-permute-start | bytes 3145736 | tf_op jit(solution)/shard_map/ppermute | solution.py:19
  279.0 36.7 %copy-start.14 = (bf16[256,2048]{1,0:T(8,128)(2,1)}, bf16[256,2048]{1,0:T(8,128)(2,1)S(1)}, u32[]{:S(2)}) copy-start(bf16[256,2048]{1,0:T(8,128)(2,1)S(1)} %collective-permute-done.1) | copy-start | bytes 3145732
  279.0 36.7 %collective-permute-start.2 = (bf16[256,2048]{1,0:T(8,128)(2,1)S(1)}, bf16[256,2048]{1,0:T(8,128)(2,1)}, u32[]{:S(2)}, u32[]{:S(2)}) collective-permute-start(bf16[256,2048]{1,0:T(8,128)(2,1)S(1)} %collective-permute-done.1), channel_id=1, source_target_pairs={{0,1},{1,2},{2,3},{3,4},{4,5},{5,6},{6,7},{7,8},{8,9},{9,10},{10,1... | collective-permute-start | bytes 3145736 | tf_op jit(solution)/shard_map/ppermute | solution.py:19
  304.5 22.5 %collective-permute-start.6 = (bf16[256,2048]{0,1:T(8,128)(2,1)}, bf16[256,2048]{0,1:T(8,128)(2,1)}, u32[]{:S(2)}, u32[]{:S(2)}) collective-permute-start(bf16[256,2048]{0,1:T(8,128)(2,1)} %collective-permute-done.5), channel_id=1, source_target_pairs={{0,1},{1,2},{2,3},{3,4},{4,5},{5,6},{6,7},{7,8},{8,9},{9,10},{10,1... | collective-permute-start | bytes 3145736 | tf_op jit(solution)/shard_map/ppermute | solution.py:19
  315.8 22.5 %collective-permute-start.3 = (bf16[256,2048]{1,0:T(8,128)(2,1)}, bf16[256,2048]{1,0:T(8,128)(2,1)}, u32[]{:S(2)}, u32[]{:S(2)}) collective-permute-start(bf16[256,2048]{1,0:T(8,128)(2,1)} %collective-permute-done.2), channel_id=1, source_target_pairs={{0,1},{1,2},{2,3},{3,4},{4,5},{5,6},{6,7},{7,8},{8,9},{9,10},{10,1... | collective-permute-start | bytes 3145736 | tf_op jit(solution)/shard_map/ppermute | solution.py:19
  319.8 1.5 copy-start.16
  319.8 1.6 copy-start.19
  323.0 19.9 %copy-start.15 = (bf16[256,2048]{1,0:T(8,128)(2,1)S(1)}, bf16[256,2048]{1,0:T(8,128)(2,1)}, u32[]{:S(2)}) copy-start(bf16[256,2048]{1,0:T(8,128)(2,1)} %copy-done.14) | copy-start | bytes 3145732
  327.0 28.2 %collective-permute-start.7 = (bf16[256,2048]{0,1:T(8,128)(2,1)}, bf16[256,2048]{0,1:T(8,128)(2,1)}, u32[]{:S(2)}, u32[]{:S(2)}) collective-permute-start(bf16[256,2048]{0,1:T(8,128)(2,1)} %collective-permute-done.6), channel_id=1, source_target_pairs={{0,1},{1,2},{2,3},{3,4},{4,5},{5,6},{6,7},{7,8},{8,9},{9,10},{10,1... | collective-permute-start | bytes 3145736 | tf_op jit(solution)/shard_map/ppermute | solution.py:19
  342.9 3.4 copy-start.11
  357.6 4.8 %copy-start.13 = (bf16[256,2048]{0,1:T(8,128)(2,1)S(1)}, bf16[256,2048]{0,1:T(8,128)(2,1)}, u32[]{:S(2)}) copy-start(bf16[256,2048]{0,1:T(8,128)(2,1)} %copy-done.12) | copy-start | bytes 3145732
  362.4 2.2 copy-start.9
  363.4 22.5 %slice-start = ((s8[5242880]{0:T(1024)(128)(4,1)}), s8[4194304]{0:T(1024)(128)(4,1)S(1)}, s32[]{:S(2)}) async-start(s8[5242880]{0:T(1024)(128)(4,1)} %bitcast.130), calls=%async_computation.3 | async-start | bytes 8388608
  364.5 21.5 %slice-start.1 = ((s8[5242880]{0:T(1024)(128)(4,1)}), s8[1048576]{0:T(1024)(128)(4,1)S(1)}, s32[]{:S(2)}) async-start(s8[5242880]{0:T(1024)(128)(4,1)} %bitcast.130), calls=%async_computation.4 | async-start | bytes 2097152
  409.8 5.3 %copy-start.1 = (f32[8,4096]{1,0:T(8,128)S(1)}, f32[8,4096]{1,0:T(8,128)}, u32[]{:S(2)}) copy-start(f32[8,4096]{1,0:T(8,128)} %param.24) | copy-start | bytes 393220
Sparse Core Ops, SparseCore 0:
  22.6 156.4 reduce-scatter.1
  223.2 79.2 all-gather.1
where the time goes:
time: 423 us; the launch traced here: 422 us
  waiting for transfers between devices  247 us (58%)
  local copies, waits for them, and re-layouts  42.9 us (10%)
  blocking collectives  39.3 us (9%)
  matrix products  33 us (8%)
  other arithmetic  27.2 us (6%)
  starting transfers between devices  17.9 us (4%)
  between operations  14.4 us (3%)
    reduce_scatter x1, waiting for transfers between devices, local(): lax.psum_scatter(jnp.concatenate([g_in, g_gate, g_out], axis=0), 'tok', s...  157 us
    ppermute x8, waiting for transfers between devices, shifted(): return lax.ppermute(block, axis, route)  90.8 us
    psum x1, blocking collectives, local(): total_power = lax.psum(power_sum, 'tok')  39.3 us
    unnamed x53, local copies, waits for them, and re-layouts  19.2 us
    ppermute x8, starting transfers between devices, shifted(): return lax.ppermute(block, axis, route)  17.8 us
    dot_general x1, matrix products, local(): jnp.einsum('qsd,ksd->sqk', noisy_tokens.reshape(row_count, sw_heads, SWDH...  12.8 us
    dot_general x1, matrix products, local(): jnp.einsum('sqk,ksd->qsd', weights.astype(jnp.bfloat16), value_window.res...  8.97 us
    concatenate x2, local copies, waits for them, and re-layouts, local(): jnp.concatenate([pair[1] for pair in earlier] + [swa_values], axis=0)  8.93 us
  transfers between devices with their start and end apart: 10, of which 8 were waited for; matrix products, arithmetic and copies ran while one was open for 15% of the time, Pallas kernels for 0%

commit v1 on v0

v1 whole, which is shorter than its diff:
```python
import functools

import jax
import jax.numpy as jnp
from jax import lax
from jax.experimental import pallas as pl
from jax.experimental.pallas import tpu as pltpu
from jax.sharding import PartitionSpec as P

SWDH = 128
WIN = 1024
BLOCK = 128

epsilon = 1e-06
update_step = 0.05


def attend_kernel(reach_ref, first_ref, q_ref, kp_ref, kc_ref, vp_ref, vc_ref, o_ref, k_all, v_all):
    b = pl.program_id(1)
    prev = kp_ref.shape[0]
    span = WIN + BLOCK

    @pl.when(b == 0)
    def _():
        k_all[:prev] = kp_ref[...]
        k_all[prev:] = kc_ref[...]
        v_all[:prev] = vp_ref[...]
        v_all[prev:] = vc_ref[...]

    start = pl.multiple_of(prev - WIN + b * BLOCK, BLOCK)
    keys = k_all[pl.ds(start, span), :]
    values = v_all[pl.ds(start, span), :]
    scores = lax.dot_general(
        q_ref[...], keys, (((1,), (1,)), ((), ())), preferred_element_type=jnp.float32
    ) * SWDH ** (-0.5)
    row = lax.broadcasted_iota(jnp.int32, (BLOCK, span), 0)
    col = lax.broadcasted_iota(jnp.int32, (BLOCK, span), 1)
    ahead = col - row
    oldest = -first_ref[0] - b * BLOCK + WIN
    visible = (ahead <= WIN) & (ahead > WIN - reach_ref[b]) & (col >= oldest)
    scores = jnp.where(visible, scores, -1e30)
    weights = jnp.exp(scores - jnp.max(scores, axis=-1, keepdims=True))
    totals = jnp.sum(weights, axis=-1, keepdims=True)
    o_ref[...] = (
        jnp.dot(weights.astype(jnp.bfloat16), values, preferred_element_type=jnp.float32) / totals
    )


def attend(reach, first, z, k_prev, k, v_prev, v, head_start, heads):
    rows = z.shape[0]
    prev = k_prev.shape[0]
    blocks = rows // BLOCK
    whole = lambda n: pl.BlockSpec((n, SWDH), lambda h, b, *_: (0, head_start + h))
    return pl.pallas_call(
        attend_kernel,
        out_shape=jax.ShapeDtypeStruct((rows, heads * SWDH), jnp.float32),
        grid_spec=pltpu.PrefetchScalarGridSpec(
            num_scalar_prefetch=2,
            grid=(heads, blocks),
            in_specs=[
                pl.BlockSpec((BLOCK, SWDH), lambda h, b, *_: (b, head_start + h)),
                whole(prev),
                whole(rows),
                whole(prev),
                whole(rows),
            ],
            out_specs=pl.BlockSpec((BLOCK, SWDH), lambda h, b, *_: (b, h)),
            scratch_shapes=[
                pltpu.VMEM((prev + rows, SWDH), jnp.bfloat16),
                pltpu.VMEM((prev + rows, SWDH), jnp.bfloat16),
            ],
        ),
        compiler_params=pltpu.CompilerParams(vmem_limit_bytes=24 * 1024 * 1024),
        cost_estimate=pl.CostEstimate(
            flops=heads * rows * (WIN + BLOCK) * SWDH * 16,
            bytes_accessed=heads * SWDH * (prev + rows) * 8,
            transcendentals=heads * rows * (WIN + BLOCK),
        ),
    )(reach, first, z, k_prev, k, v_prev, v)


def local(
    clean_keys,
    clean_values,
    clean_rates,
    w_in,
    w_gate,
    w_out,
    noisy_tokens,
    swa_keys,
    swa_values,
    level_ids,
    window_reach,
    level_mod,
    mem_gain,
):
    count = clean_keys.shape[0]
    heads, size = w_in.shape[0], w_in.shape[1]
    flat = heads * size
    frames = level_ids.shape[0]
    devices = lax.axis_size("tok")
    position = lax.axis_index("tok")
    mine = position % heads
    group = position // heads
    rows = heads * count
    bf16, f32 = jnp.bfloat16, jnp.float32
    peers = [[g * heads + h for g in range(devices // heads)] for h in range(heads)]

    def swap(block, s):
        return lax.ppermute(block, "tok", [(i, i ^ s) for i in range(devices)])

    def columns(array, head):
        return lax.dynamic_slice_in_dim(array, head * size, size, 1)

    rates = jnp.repeat(clean_rates, size, axis=1)
    scaled_rows = (rates * clean_values.astype(f32)).astype(bf16)
    clean = []
    for s in range(heads):
        piece = jnp.stack([columns(clean_keys, mine ^ s), columns(scaled_rows, mine ^ s)])
        clean.append(piece if s == 0 else swap(piece, s))
    keys = jnp.concatenate([p[0] for p in clean], axis=0)
    scaled = jnp.concatenate([p[1] for p in clean], axis=0)

    square = jnp.mean(jnp.square(noisy_tokens.astype(f32)), axis=-1)
    own = jnp.concatenate([square, level_ids.astype(f32), window_reach.astype(f32)])[None, :]
    facts = jnp.zeros((heads, own.shape[1]), f32)
    for s in range(heads):
        piece = own if s == 0 else swap(own, s)
        facts = lax.dynamic_update_slice(facts, piece, (mine ^ s, 0))

    noisy = jnp.zeros((3, rows, size), bf16)
    for s in range(heads):
        piece = jnp.stack([columns(a, mine ^ s) for a in (noisy_tokens, swa_keys, swa_values)])
        piece = piece if s == 0 else swap(piece, s)
        noisy = lax.dynamic_update_slice(noisy, piece, (0, (mine ^ s) * count, 0))
    z = noisy[0]
    kv = noisy[1:]
    earlier = []
    carried = kv
    for hop in range(-(-WIN // rows)):
        carried = lax.ppermute(
            carried, "tok", [(i, i + heads) for i in range(devices - heads)]
        )
        earlier.insert(0, carried)
    before = earlier[0] if len(earlier) == 1 else jnp.concatenate(earlier, axis=1)

    base = [lax.dynamic_index_in_dim(w, mine, 0, keepdims=False) for w in (w_in, w_gate, w_out)]
    dot = functools.partial(lax.dot_general, preferred_element_type=f32)
    nt, nn, tn = (((1,), (1,)), ((), ())), (((1,), (0,)), ((), ())), (((0,), (0,)), ((), ()))
    first = dot(keys, base[0], nt)
    second = dot(keys, base[1], nt)
    sigmoid = jax.nn.sigmoid(first)
    active = first * sigmoid
    hidden = (active * second).astype(bf16)
    d_act = dot(scaled, base[2], nn)
    d_first = (d_act * second * sigmoid * (1.0 + first * (1.0 - sigmoid))).astype(bf16)
    d_second = (d_act * active).astype(bf16)
    grads = jnp.concatenate(
        [dot(d_first, keys, tn), dot(d_second, keys, tn), dot(scaled, hidden, tn)], axis=0
    )
    share = lax.psum_scatter(
        grads, "tok", scatter_dimension=0, tiled=True, axis_index_groups=peers
    )
    grad = lax.all_gather(
        share.astype(bf16), "tok", axis=0, tiled=True, axis_index_groups=peers
    ).astype(f32)
    own_power = jnp.broadcast_to(jnp.sum(grad * grad), (8, 128))
    power = own_power
    for s in range(1, heads):
        power = power + swap(own_power, s)

    reach = facts[:, count + frames :].reshape(-1).astype(jnp.int32)
    first_token = (group * rows).astype(jnp.int32).reshape(1)
    half = size // SWDH // 2
    attended = jnp.concatenate(
        [
            attend(reach, first_token, z, before[0], kv[0], before[1], kv[1], start, half)
            for start in (0, half)
        ],
        axis=1,
    )

    grad_scale = lax.rsqrt(power[0, 0] / (3 * flat * size) + epsilon)
    initial = jnp.concatenate(base, axis=0).astype(f32)
    update = initial + update_step * grad * grad_scale
    target = jnp.sqrt(jnp.mean(initial * initial, axis=-1, keepdims=True))
    memory = (
        update * target * lax.rsqrt(jnp.mean(update * update, axis=-1, keepdims=True) + epsilon)
    ).astype(bf16)

    inverse = lax.rsqrt(facts[:, :count].reshape(rows, 1) + epsilon)
    levels = facts[:, count : count + frames].reshape(-1).astype(jnp.int32)
    scale = jnp.take(columns(level_mod[:, :flat], mine), levels, axis=0)
    shift = jnp.take(columns(level_mod[:, flat:], mine), levels, axis=0)
    queries = (
        (z.astype(f32) * inverse).reshape(-1, BLOCK, size) * (1.0 + scale[:, None, :])
        + shift[:, None, :]
    ).astype(bf16).reshape(rows, size)
    mixture = (
        jax.nn.silu(dot(queries, memory[:size], nt)) * dot(queries, memory[size : 2 * size], nt)
    ).astype(bf16)
    recalled = dot(mixture, memory[2 * size :], nt)
    gain = lax.dynamic_slice_in_dim(mem_gain, mine * size, size, 0)
    recalled = (
        recalled * lax.rsqrt(jnp.mean(recalled * recalled, axis=-1, keepdims=True) + epsilon) * gain
    )
    done = (recalled + attended).astype(bf16)
    result = jnp.zeros((count, flat), bf16)
    for s in range(heads):
        piece = lax.dynamic_slice_in_dim(done, (mine ^ s) * count, count, 0)
        piece = piece if s == 0 else swap(piece, s)
        result = lax.dynamic_update_slice(result, piece, (0, (mine ^ s) * size))
    return result


def solution(mesh):
    rows = P(("groups", "tok"), None)
    blocks = P(("groups", "tok"))
    return jax.shard_map(
        local,
        mesh=mesh,
        in_specs=(rows, rows, rows, P(), P(), P(), rows, rows, rows, blocks, blocks, P(), P()),
        out_specs=rows,
        check_vma=False,
    )
```

time: 423 us -> 248 us (0.59)
  waiting for transfers between devices: 247 us -> 121 us
  blocking collectives: 39.3 us -> 0 us
  Pallas kernels: 0 us -> 24.8 us
  matrix products: 33 us -> 11.8 us
  local copies, waits for them, and re-layouts: 42.9 us -> 36.7 us
  other arithmetic: 27.2 us -> 22.8 us
  starting transfers between devices: 17.9 us -> 13.5 us
    reduce_scatter x1, waiting for transfers between devices: 157 us -> 30.1 us  [local(): lax.psum_scatter(grads, 'tok', scatter_dimension=0, tiled=True, axis_inde...]
    psum x1 -> x0, blocking collectives: 39.3 us -> none  [local(): total_power = lax.psum(power_sum, 'tok')]
    pallas_call x0 -> x2, Pallas kernels: none -> 24.8 us  [attend(): pl.pallas_call(attend_kernel, out_shape=jax.ShapeDtypeStruct((rows, heads...]
    dot_general x11 -> x8, matrix products: 33 us -> 11.8 us  [the longest x1 4.64 us: local(): recalled = dot(mixture, memory[2 * size:], nt)]
    concatenate x3 -> x0, local copies, waits for them, and re-layouts: 10 us -> none  [the longest x2 8.93 us: local(): jnp.concatenate([pair[1] for pair in earlier] + [swa_values], axis=0)]
    reduce_sum x4 -> x3, other arithmetic: 12.1 us -> 4.21 us  [the longest x1 3.02 us: local(): own_power = jnp.broadcast_to(jnp.sum(grad * grad), (8, 128))]
    squeeze x0 -> x7, local copies, waits for them, and re-layouts: none -> 6.74 us  [the longest x1 2.06 us: local(): kv[1]]
    unnamed x53 -> x63, local copies, waits for them, and re-layouts: 19.2 us -> 13.6 us
  transfers between devices with their start and end apart: 10 -> 18, of which waited for: 8 -> 9; matrix products, arithmetic and copies ran while one was open for 15% -> 10% of each run, Pallas kernels for 0% -> 10%
where the time goes in v1:
time: 248 us; the launch traced here: 245 us
  waiting for transfers between devices  121 us (49%)
  local copies, waits for them, and re-layouts  36.7 us (15%)
  Pallas kernels  24.8 us (10%)
  other arithmetic  22.8 us (9%)
  between operations  14.8 us (6%)
  starting transfers between devices  13.5 us (5%)
  matrix products  11.8 us (5%)
    ppermute x15, waiting for transfers between devices, swap(): return lax.ppermute(block, 'tok', [(i, i ^ s) for i in range(devices)])  59.8 us
    reduce_scatter x1, waiting for transfers between devices, local(): lax.psum_scatter(grads, 'tok', scatter_dimension=0, tiled=True, axis_inde...  30.1 us
    ppermute x1, waiting for transfers between devices, local(): lax.ppermute(carried, 'tok', [(i, i + heads) for i in range(devices - hea...  27.4 us
    pallas_call x2, Pallas kernels, attend(): pl.pallas_call(attend_kernel, out_shape=jax.ShapeDtypeStruct((rows, heads...  24.8 us
    unnamed x63, local copies, waits for them, and re-layouts  13.6 us
    ppermute x15, starting transfers between devices, swap(): return lax.ppermute(block, 'tok', [(i, i ^ s) for i in range(devices)])  10 us
  transfers between devices with their start and end apart: 18, of which 9 were waited for; matrix products, arithmetic and copies ran while one was open for 10% of the time, Pallas kernels for 10%

profile of v1, /device:TPU:8, one launch (start us, length us, event | category | flops | bytes accessed | tf_op | source)
XLA Modules:
  0.0 245.2 jit_solution(13716152626714858565)
XLA Ops:
  7.9 2.2 copy.19
  10.1 2.0 multiply_convert_fusion.5
  14.7 1.5 collective-permute-start.7
  17.4 1.3 dynamic-slice_bitcast_fusion
  18.8 1.6 slice_bitcast_fusion.10
  20.4 9.2 %collective-permute-done.7 = bf16[2,256,512]{2,1,0:T(8,128)(2,1)S(1)} collective-permute-done((bf16[2,256,512]{2,1,0:T(8,128)(2,1)}, bf16[2,256,512]{2,1,0:T(8,128)(2,1)S(1)}, u32[]{:S(2)}, u32[]{:S(2)}) %collective-permute-start.7) | collective-permute-done | bytes 524320 | tf_op jit(solution)/shard_map/ppermute | solution.py:110
  29.7 10.4 %collective-permute-done.8 = bf16[2,256,512]{2,1,0:T(8,128)(2,1)S(1)} collective-permute-done((bf16[2,256,512]{2,1,0:T(8,128)(2,1)}, bf16[2,256,512]{2,1,0:T(8,128)(2,1)S(1)}, u32[]{:S(2)}, u32[]{:S(2)}) %collective-permute-start.8) | collective-permute-done | bytes 524320 | tf_op jit(solution)/shard_map/ppermute | solution.py:110
  43.2 1.3 fusion.9
  45.4 2.0 pad_maximum_fusion
  47.4 1.1 copy-done.18
  48.9 2.1 dynamic-slice_bitcast_fusion.9
  51.0 1.0 pad_maximum_fusion.4
  52.3 1.6 collective-permute-start.1
  53.8 1.0 pad_maximum_fusion.6
  55.9 1.5 collective-permute-start.4
  57.8 1.2 constant_dynamic-update-slice_fusion.5
  59.0 13.8 %collective-permute-done.1 = bf16[3,256,512]{2,1,0:T(8,128)(2,1)} collective-permute-done((bf16[3,256,512]{2,1,0:T(8,128)(2,1)S(1)}, bf16[3,256,512]{2,1,0:T(8,128)(2,1)}, u32[]{:S(2)}, u32[]{:S(2)}) %collective-permute-start.1) | collective-permute-done | bytes 786464 | tf_op jit(solution)/shard_map/ppermute | solution.py:110
  72.8 1.2 constant_dynamic-update-slice_fusion.4
  74.0 14.4 %collective-permute-done.2 = bf16[3,256,512]{2,1,0:T(8,128)(2,1)} collective-permute-done((bf16[3,256,512]{2,1,0:T(8,128)(2,1)}, bf16[3,256,512]{2,1,0:T(8,128)(2,1)}, u32[]{:S(2)}, u32[]{:S(2)}) %collective-permute-start.2) | collective-permute-done | bytes 786464 | tf_op jit(solution)/shard_map/ppermute | solution.py:110
  88.4 1.2 constant_dynamic-update-slice_fusion.3
  89.6 1.5 slice.107
  92.0 3.4 %collective-permute-start.12 = (bf16[2,1024,512]{2,1,0:T(8,128)(2,1)}, bf16[2,1024,512]{2,1,0:T(8,128)(2,1)}, u32[]{:S(2)}, u32[]{:S(2)}) collective-permute-start(bf16[2,1024,512]{2,1,0:T(8,128)(2,1)} %slice.107), channel_id=1, source_target_pairs={{0,4},{1,5},{2,6},{3,7},{4,8},{5,9},{6,10},{7,11},{8,12},{9,13},{1... | collective-permute-start | bytes 6291464 | tf_op jit(solution)/shard_map/ppermute | solution.py:141
  95.5 30.1 %reduce-scatter.2.cloned.1.call-done = f32[192,512]{1,0:T(8,128)} async-done(((f32[1536,512]{1,0:T(8,128)}), f32[192,512]{1,0:T(8,128)}) %reduce-scatter.2.cloned.1.call-update) | async-done | bytes 393232 | tf_op jit(solution)/shard_map/reduce_scatter | solution.py:161
  125.6 1.7 convert_element_type.75
  130.0 2.6 %fusion.3 = bf16[1024,512]{1,0:T(8,128)(2,1)} fusion(f32[8,512]{1,0:T(8,128)S(1)} %get-tuple-element.48, f32[8,512]{1,0:T(8,128)S(1)} %get-tuple-element.47, f32[1024]{0:T(1024)S(1)} %bitcast.88, bf16[3,1024,512]{2,1,0:T(8,128)(2,1)} %copy-done.10), kind=kLoop, calls=%fused_computation.14 | loop fusion | flops 2621440 | bytes 2134016 | tf_op jit(solution)/shard_map/convert_element_type | solution.py:198
  132.6 2.1 slice_bitcast_fusion
  134.7 27.4 %collective-permute-done.12 = bf16[2,1024,512]{2,1,0:T(8,128)(2,1)} collective-permute-done((bf16[2,1024,512]{2,1,0:T(8,128)(2,1)}, bf16[2,1024,512]{2,1,0:T(8,128)(2,1)}, u32[]{:S(2)}, u32[]{:S(2)}) %collective-permute-start.12) | collective-permute-done | bytes 2097184 | tf_op jit(solution)/shard_map/ppermute | solution.py:141
  162.1 1.7 slice_bitcast_fusion.1
  163.8 12.3 %shard_map.127 = f32[1024,256]{1,0:T(8,128)S(1)} custom-call(s32[8]{0:T(128)S(1)} %convert_element_type.80.reach_ref, s32[1]{0:T(128)} %bitcast.31.first_ref, bf16[1024,512]{1,0:T(8,128)(2,1)S(1)} %get-tuple-element.10.q_ref, bf16[1024,512]{1,0:T(8,128)(2,1)S(1)} %get-tuple-element.12.kp_ref, bf16[1024,512]{1,0:T(8,128)(2,1)S(1)} %get-tuple-element.9.kc_ref, ...), custom_call_target="tpu_custom_call" | custom-call | flops 4831838208 | bytes 4194304 | tf_op jit(solution)/shard_map/pallas_call | solution.py:54
  176.2 1.0 copy-done.6
  177.1 1.0 copy-done.8
  178.2 3.5 %all-gather.2.cloned.1.call-done = bf16[1536,512]{1,0:T(8,128)(2,1)} async-done(((bf16[192,512]{1,0:T(8,128)(2,1)}), bf16[1536,512]{1,0:T(8,128)(2,1)}) %all-gather.2.cloned.1.call-update) | async-done | bytes 1572880 | tf_op jit(solution)/shard_map/all_gather | solution.py:164
  181.7 3.0 %fusion.1 = f32[]{:T(128)} fusion(bf16[1536,512]{1,0:T(8,128)(2,1)} %all-gather.2.cloned.1.call-done), kind=kLoop, calls=%fused_computation.7 | loop fusion | flops 2359295 | bytes 1572868 | tf_op jit(solution)/shard_map/reduce_sum | solution.py:167
  185.4 1.5 collective-permute-start.10
  187.6 1.2 copy-done.3
  188.8 1.2 copy-done.5
  190.1 1.2 copy-done.7
  191.3 1.2 copy-done.9
  192.5 12.5 %shard_map.128 = f32[1024,256]{1,0:T(8,128)S(1)} custom-call(s32[8]{0:T(128)S(1)} %convert_element_type.80.reach_ref, s32[1]{0:T(128)} %bitcast.31.first_ref, bf16[1024,512]{1,0:T(8,128)(2,1)S(1)} %copy-done.5, bf16[1024,512]{1,0:T(8,128)(2,1)S(1)} %copy-done.9, bf16[1024,512]{1,0:T(8,128)(2,1)S(1)} %copy-done.3, bf16[1024,512]{1,0:T(8,128)(2,1)S(1)} %copy-done.7, ...), custom_call_target="tpu_custom_call" | custom-call | flops 4831838208 | bytes 4194304 | tf_op jit(solution)/shard_map/pallas_call | solution.py:54
  207.9 2.8 %multiply_convert_fusion = bf16[1536,512]{1,0:T(8,128)(2,1)S(1)} fusion(bf16[1536,512]{1,0:T(8,128)(2,1)S(1)} %copy-done.11, f32[1536]{0:T(1024)S(1)} %add_rsqrt_fusion, f32[1536]{0:T(1024)S(1)} %multiply_sqrt_fusion, f32[]{:T(128)} %bitcast.30, bf16[512,512]{1,0:T(8,128)(2,1)S(1)} %copy-done.13, bf16[512,512]{1,0:T(8,128)(2,1)S(1)} %copy-done.15, ...), kind=kLoop, calls=%fused_computation.9 | loop fusion | flops 9437184 | bytes 4730884 | tf_op jit(solution)/shard_map/convert_element_type | solution.py:189
  210.8 1.2 copy-done.20
  211.9 2.1 fusion.13
  214.0 4.6 %multiply_reduce_fusion.1 = (f32[1024]{0:T(1024)S(1)}, f32[1024,512]{0,1:T(8,128)}) fusion(bf16[1536,512]{1,0:T(8,128)(2,1)} %copy-done.20, f32[1024,512]{1,0:T(8,128)} %fusion.13, bf16[1024,512]{1,0:T(8,128)(2,1)S(1)} %copy-done.19), kind=kOutput, calls=%fused_computation.16 | convolution fusion | flops 1077935104 | bytes 6295552 | tf_op jit(solution)/shard_map/dot_general | solution.py:202
  218.7 2.9 %copy.17 = f32[1024,512]{1,0:T(8,128)} copy(f32[1024,512]{0,1:T(8,128)} %get-tuple-element.50) | data formatting | bytes 4194304 | tf_op jit(solution)/shard_map/dot_general | solution.py:202
  221.5 1.9 fusion.2
  223.8 1.5 collective-permute-start.14
  225.7 7.3 %collective-permute-done.14 = bf16[256,512]{1,0:T(8,128)(2,1)S(1)} collective-permute-done((bf16[256,512]{1,0:T(8,128)(2,1)S(1)}, bf16[256,512]{1,0:T(8,128)(2,1)S(1)}, u32[]{:S(2)}, u32[]{:S(2)}) %collective-permute-start.14) | collective-permute-done | bytes 262176 | tf_op jit(solution)/shard_map/ppermute | solution.py:110
  233.0 4.7 %collective-permute-done.15 = bf16[256,512]{1,0:T(8,128)(2,1)S(1)} collective-permute-done((bf16[256,512]{1,0:T(8,128)(2,1)S(1)}, bf16[256,512]{1,0:T(8,128)(2,1)S(1)}, u32[]{:S(2)}, u32[]{:S(2)}) %collective-permute-start.15) | collective-permute-done | bytes 262176 | tf_op jit(solution)/shard_map/ppermute | solution.py:110
  (130 shorter events, 19.7 us)
Async XLA Ops:
  6.5 12.2 %copy-start = (bf16[4,512,512]{2,1,0:T(8,128)(2,1)S(1)}, bf16[4,512,512]{2,1,0:T(8,128)(2,1)}, u32[]{:S(2)}) copy-start(bf16[4,512,512]{2,1,0:T(8,128)(2,1)} %param.18) | copy-start | bytes 6291460
  6.5 119.0 %reduce-scatter.2.cloned.1.call-start = ((), (), s32[]{:S(2)}) async-start(), calls=%async_computation.1 | async-start | bytes 3538944 | tf_op jit(solution)/shard_map/reduce_scatter | solution.py:161
  7.9 2.3 copy-start.22
  10.1 2.0 copy-start.23
  13.9 4.9 %collective-permute-start.6 = (bf16[2,256,512]{2,1,0:T(8,128)(2,1)}, bf16[2,256,512]{2,1,0:T(8,128)(2,1)}, u32[]{:S(2)}, u32[]{:S(2)}) collective-permute-start(bf16[2,256,512]{2,1,0:T(8,128)(2,1)} %pad_maximum_fusion.7), channel_id=1, source_target_pairs={{0,1},{1,0},{2,3},{3,2},{4,5},{5,4},{6,7},{7,6},{8,9},{9,8},{10,11... | collective-permute-start | bytes 1572872 | tf_op jit(solution)/shard_map/ppermute | solution.py:110
  14.7 14.9 %collective-permute-start.7 = (bf16[2,256,512]{2,1,0:T(8,128)(2,1)}, bf16[2,256,512]{2,1,0:T(8,128)(2,1)S(1)}, u32[]{:S(2)}, u32[]{:S(2)}) collective-permute-start(bf16[2,256,512]{2,1,0:T(8,128)(2,1)} %pad_maximum_fusion.8), channel_id=1, source_target_pairs={{0,2},{1,3},{2,0},{3,1},{4,6},{5,7},{6,4},{7,5},{8,10},{9,11},{10,... | collective-permute-start | bytes 1572872 | tf_op jit(solution)/shard_map/ppermute | solution.py:110
  17.1 23.1 %collective-permute-start.8 = (bf16[2,256,512]{2,1,0:T(8,128)(2,1)}, bf16[2,256,512]{2,1,0:T(8,128)(2,1)S(1)}, u32[]{:S(2)}, u32[]{:S(2)}) collective-permute-start(bf16[2,256,512]{2,1,0:T(8,128)(2,1)} %pad_maximum_fusion.9), channel_id=1, source_target_pairs={{0,3},{1,2},{2,1},{3,0},{4,7},{5,6},{6,5},{7,4},{8,11},{9,10},{10,... | collective-permute-start | bytes 1572872 | tf_op jit(solution)/shard_map/ppermute | solution.py:110
  18.7 22.2 %copy-start.14 = (bf16[512,512]{1,0:T(8,128)(2,1)}, bf16[512,512]{1,0:T(8,128)(2,1)S(1)}, u32[]{:S(2)}) copy-start(bf16[512,512]{1,0:T(8,128)(2,1)S(1)} %get-tuple-element.52) | copy-start | bytes 1572868
  18.7 23.0 %copy-start.12 = (bf16[512,512]{1,0:T(8,128)(2,1)}, bf16[512,512]{1,0:T(8,128)(2,1)S(1)}, u32[]{:S(2)}) copy-start(bf16[512,512]{1,0:T(8,128)(2,1)S(1)} %get-tuple-element.51) | copy-start | bytes 1572868
  18.7 21.4 %copy-start.26 = (bf16[256,512]{1,0:T(8,128)(2,1)S(1)}, bf16[256,512]{1,0:T(8,128)(2,1)}, u32[]{:S(2)}) copy-start(bf16[256,512]{1,0:T(8,128)(2,1)} %get-tuple-element.21) | copy-start | bytes 786436
  18.8 22.1 %copy-start.16 = (bf16[512,512]{1,0:T(8,128)(2,1)}, bf16[512,512]{1,0:T(8,128)(2,1)S(1)}, u32[]{:S(2)}) copy-start(bf16[512,512]{1,0:T(8,128)(2,1)S(1)} %dynamic-slice_bitcast_fusion.2) | copy-start | bytes 1572868
  47.4 1.2 copy-start.18
  47.4 1.5 copy-start.24
  47.4 134.3 %all-gather.2.cloned.1.call-start = ((), (), s32[]{:S(2)}) async-start(), calls=%async_computation.2 | async-start | bytes 1769472 | tf_op jit(solution)/shard_map/all_gather | solution.py:164
  52.0 5.8 %collective-permute-start = (bf16[3,256,512]{2,1,0:T(8,128)(2,1)}, bf16[3,256,512]{2,1,0:T(8,128)(2,1)}, u32[]{:S(2)}, u32[]{:S(2)}) collective-permute-start(bf16[3,256,512]{2,1,0:T(8,128)(2,1)} %pad_maximum_fusion.4), channel_id=1, source_target_pairs={{0,1},{1,0},{2,3},{3,2},{4,5},{5,4},{6,7},{7,6},{8,9},{9,8},{10,11... | collective-permute-start | bytes 2359304 | tf_op jit(solution)/shard_map/ppermute | solution.py:110
  52.2 3.1 %copy-start.28 = (s32[2]{0:T(128)S(1)}, s32[2]{0:T(128)}, u32[]{:S(2)}) copy-start(s32[2]{0:T(128)} %param.24) | copy-start | bytes 28
  52.2 3.1 %copy-start.29 = (s32[2]{0:T(128)S(1)}, s32[2]{0:T(128)}, u32[]{:S(2)}) copy-start(s32[2]{0:T(128)} %param.25) | copy-start | bytes 28
  52.3 20.5 %collective-permute-start.1 = (bf16[3,256,512]{2,1,0:T(8,128)(2,1)S(1)}, bf16[3,256,512]{2,1,0:T(8,128)(2,1)}, u32[]{:S(2)}, u32[]{:S(2)}) collective-permute-start(bf16[3,256,512]{2,1,0:T(8,128)(2,1)S(1)} %pad_maximum_fusion.5), channel_id=1, source_target_pairs={{0,2},{1,3},{2,0},{3,1},{4,6},{5,7},{6,4},{7,5},{8,10},{9,11},{10,... | collective-permute-start | bytes 2359304 | tf_op jit(solution)/shard_map/ppermute | solution.py:110
  54.8 2.8 %copy-start.25 = (bf16[1,256,512]{2,1,0:T(8,128)(2,1)S(1)}, bf16[1,256,512]{2,1,0:T(8,128)(2,1)}, u32[]{:S(2)}) copy-start(bf16[1,256,512]{2,1,0:T(8,128)(2,1)} %get-tuple-element.54) | copy-start | bytes 786436
  54.8 33.6 %collective-permute-start.2 = (bf16[3,256,512]{2,1,0:T(8,128)(2,1)}, bf16[3,256,512]{2,1,0:T(8,128)(2,1)}, u32[]{:S(2)}, u32[]{:S(2)}) collective-permute-start(bf16[3,256,512]{2,1,0:T(8,128)(2,1)} %pad_maximum_fusion.6), channel_id=1, source_target_pairs={{0,3},{1,2},{2,1},{3,0},{4,7},{5,6},{6,5},{7,4},{8,11},{9,10},{10,... | collective-permute-start | bytes 2359304 | tf_op jit(solution)/shard_map/ppermute | solution.py:110
  55.4 72.8 %collective-permute-start.3 = (f32[1,260]{1,0:T(1,128)S(1)}, f32[1,260]{1,0:T(1,128)S(1)}, u32[]{:S(2)}, u32[]{:S(2)}) collective-permute-start(f32[1,260]{1,0:T(1,128)S(1)} %broadcast_in_dim.36), channel_id=1, source_target_pairs={{0,1},{1,0},{2,3},{3,2},{4,5},{5,4},{6,7},{7,6},{8,9},{9,8},{10,11... | collective-permute-start | bytes 3128 | tf_op jit(solution)/shard_map/ppermute | solution.py:110
  55.9 72.3 %collective-permute-start.4 = (f32[1,260]{1,0:T(1,128)S(1)}, f32[1,260]{1,0:T(1,128)S(1)}, u32[]{:S(2)}, u32[]{:S(2)}) collective-permute-start(f32[1,260]{1,0:T(1,128)S(1)} %broadcast_in_dim.36), channel_id=1, source_target_pairs={{0,2},{1,3},{2,0},{3,1},{4,6},{5,7},{6,4},{7,5},{8,10},{9,11},{10,... | collective-permute-start | bytes 3128 | tf_op jit(solution)/shard_map/ppermute | solution.py:110
  57.7 70.5 %collective-permute-start.5 = (f32[1,260]{1,0:T(1,128)S(1)}, f32[1,260]{1,0:T(1,128)S(1)}, u32[]{:S(2)}, u32[]{:S(2)}) collective-permute-start(f32[1,260]{1,0:T(1,128)S(1)} %broadcast_in_dim.36), channel_id=1, source_target_pairs={{0,3},{1,2},{2,1},{3,0},{4,7},{5,6},{6,5},{7,4},{8,11},{9,10},{10,... | collective-permute-start | bytes 3128 | tf_op jit(solution)/shard_map/ppermute | solution.py:110
  89.6 2.4 copy-start.10
  89.6 37.7 %copy-start.27 = (f32[8,4096]{1,0:T(8,128)S(1)}, f32[8,4096]{1,0:T(8,128)}, u32[]{:S(2)}) copy-start(f32[8,4096]{1,0:T(8,128)} %param.26) | copy-start | bytes 393220
  92.0 70.1 %collective-permute-start.12 = (bf16[2,1024,512]{2,1,0:T(8,128)(2,1)}, bf16[2,1024,512]{2,1,0:T(8,128)(2,1)}, u32[]{:S(2)}, u32[]{:S(2)}) collective-permute-start(bf16[2,1024,512]{2,1,0:T(8,128)(2,1)} %slice.107), channel_id=1, source_target_pairs={{0,4},{1,5},{2,6},{3,7},{4,8},{5,9},{6,10},{7,11},{8,12},{9,13},{1... | collective-permute-start | bytes 6291464 | tf_op jit(solution)/shard_map/ppermute | solution.py:141
  134.6 29.1 %copy-start.2 = (bf16[1024,512]{1,0:T(8,128)(2,1)}, bf16[1024,512]{1,0:T(8,128)(2,1)S(1)}, u32[]{:S(2)}) copy-start(bf16[1024,512]{1,0:T(8,128)(2,1)S(1)} %get-tuple-element.9.kc_ref) | copy-start | bytes 3145732
  134.7 29.1 %copy-start.4 = (bf16[1024,512]{1,0:T(8,128)(2,1)}, bf16[1024,512]{1,0:T(8,128)(2,1)S(1)}, u32[]{:S(2)}) copy-start(bf16[1024,512]{1,0:T(8,128)(2,1)S(1)} %get-tuple-element.10.q_ref) | copy-start | bytes 3145732
  176.1 1.0 copy-start.6
  177.1 1.0 copy-start.8
  181.7 25.2 %copy-start.11 = (bf16[1536,512]{1,0:T(8,128)(2,1)S(1)}, bf16[1536,512]{1,0:T(8,128)(2,1)}, u32[]{:S(2)}) copy-start(bf16[1536,512]{1,0:T(8,128)(2,1)} %all-gather.2.cloned.1.call-done) | copy-start | bytes 4718596
  185.4 19.6 %collective-permute-start.10 = (f32[8,128]{1,0:T(8,128)S(1)}, f32[8,128]{1,0:T(8,128)S(1)}, u32[]{:S(2)}, u32[]{:S(2)}) collective-permute-start(f32[8,128]{1,0:T(8,128)S(1)} %broadcast_in_dim.38), channel_id=1, source_target_pairs={{0,2},{1,3},{2,0},{3,1},{4,6},{5,7},{6,4},{7,5},{8,10},{9,11},{10,... | collective-permute-start | bytes 12296 | tf_op jit(solution)/shard_map/ppermute | solution.py:110
  186.9 18.1 %collective-permute-start.11 = (f32[8,128]{1,0:T(8,128)S(1)}, f32[8,128]{1,0:T(8,128)S(1)}, u32[]{:S(2)}, u32[]{:S(2)}) collective-permute-start(f32[8,128]{1,0:T(8,128)S(1)} %broadcast_in_dim.38), channel_id=1, source_target_pairs={{0,3},{1,2},{2,1},{3,0},{4,7},{5,6},{6,5},{7,4},{8,11},{9,10},{10,... | collective-permute-start | bytes 12296 | tf_op jit(solution)/shard_map/ppermute | solution.py:110
  186.9 18.1 %collective-permute-start.9 = (f32[8,128]{1,0:T(8,128)S(1)}, f32[8,128]{1,0:T(8,128)S(1)}, u32[]{:S(2)}, u32[]{:S(2)}) collective-permute-start(f32[8,128]{1,0:T(8,128)S(1)} %broadcast_in_dim.38), channel_id=1, source_target_pairs={{0,1},{1,0},{2,3},{3,2},{4,5},{5,4},{6,7},{7,6},{8,9},{9,8},{10,11... | collective-permute-start | bytes 12296 | tf_op jit(solution)/shard_map/ppermute | solution.py:110
  187.6 1.2 copy-start.3
  188.8 1.2 copy-start.5
  190.1 1.2 copy-start.7
  191.3 1.2 copy-start.9
  192.5 14.4 %copy-start.13 = (bf16[512,512]{1,0:T(8,128)(2,1)S(1)}, bf16[512,512]{1,0:T(8,128)(2,1)}, u32[]{:S(2)}) copy-start(bf16[512,512]{1,0:T(8,128)(2,1)} %copy-done.12) | copy-start | bytes 1572868
  192.5 14.4 %copy-start.15 = (bf16[512,512]{1,0:T(8,128)(2,1)S(1)}, bf16[512,512]{1,0:T(8,128)(2,1)}, u32[]{:S(2)}) copy-start(bf16[512,512]{1,0:T(8,128)(2,1)} %copy-done.14) | copy-start | bytes 1572868
  192.5 14.4 %copy-start.17 = (bf16[512,512]{1,0:T(8,128)(2,1)S(1)}, bf16[512,512]{1,0:T(8,128)(2,1)}, u32[]{:S(2)}) copy-start(bf16[512,512]{1,0:T(8,128)(2,1)} %copy-done.16) | copy-start | bytes 1572868
  207.9 4.0 %copy-start.19 = (bf16[1024,512]{1,0:T(8,128)(2,1)S(1)}, bf16[1024,512]{1,0:T(8,128)(2,1)}, u32[]{:S(2)}) copy-start(bf16[1024,512]{1,0:T(8,128)(2,1)} %fusion.3) | copy-start | bytes 3145732
  210.8 1.2 copy-start.20
  223.5 14.9 %copy-start.1 = (bf16[4,512,512]{2,1,0:T(8,128)(2,1)S(1)}, bf16[4,512,512]{2,1,0:T(8,128)(2,1)}, u32[]{:S(2)}) copy-start(bf16[4,512,512]{2,1,0:T(8,128)(2,1)} %param.18) | copy-start | bytes 6291460
  223.7 1.9 collective-permute-start.13
  223.8 9.2 %collective-permute-start.14 = (bf16[256,512]{1,0:T(8,128)(2,1)S(1)}, bf16[256,512]{1,0:T(8,128)(2,1)S(1)}, u32[]{:S(2)}, u32[]{:S(2)}) collective-permute-start(bf16[256,512]{1,0:T(8,128)(2,1)S(1)} %get-tuple-element.14), channel_id=1, source_target_pairs={{0,2},{1,3},{2,0},{3,1},{4,6},{5,7},{6,4},{7,5},{8,10},{9,11},{10,... | collective-permute-start | bytes 786440 | tf_op jit(solution)/shard_map/ppermute | solution.py:110
  225.3 12.4 %collective-permute-start.15 = (bf16[256,512]{1,0:T(8,128)(2,1)S(1)}, bf16[256,512]{1,0:T(8,128)(2,1)S(1)}, u32[]{:S(2)}, u32[]{:S(2)}) collective-permute-start(bf16[256,512]{1,0:T(8,128)(2,1)S(1)} %get-tuple-element.13), channel_id=1, source_target_pairs={{0,3},{1,2},{2,1},{3,0},{4,7},{5,6},{6,5},{7,4},{8,11},{9,10},{10,... | collective-permute-start | bytes 786440 | tf_op jit(solution)/shard_map/ppermute | solution.py:110
  233.0 4.7 %copy-start.21 = (bf16[256,2048]{1,0:T(8,128)(2,1)}, bf16[256,2048]{1,0:T(8,128)(2,1)S(1)}, u32[]{:S(2)}) copy-start(bf16[256,2048]{1,0:T(8,128)(2,1)S(1)} %constant_dynamic-update-slice_fusion.1) | copy-start | bytes 3145732
Sparse Core Ops, SparseCore 0:
  47.5 78.0 reduce-scatter.1
  127.7 53.8 all-gather.1

commit v2 on v1

--- a/solution.py
+++ b/solution.py
@@ -104,10 +104,18 @@
     group = position // heads
     rows = heads * count
     bf16, f32 = jnp.bfloat16, jnp.float32
-    peers = [[g * heads + h for g in range(devices // heads)] for h in range(heads)]
+    assert heads == 4 and devices % 8 == 0
+
+    def crossed(i):
+        return (i & ~6) | ((i & 2) << 1) | ((i & 4) >> 1)
+
+    every = range(devices)
+    peers = [[i for i in every if i % heads == h] for h in range(heads)]
+    clean_peers = [[i for i in every if crossed(i) % heads == h] for h in range(heads)]
+    clean_mine = (position & 1) | ((position >> 1) & 2)
 
     def swap(block, s):
-        return lax.ppermute(block, "tok", [(i, i ^ s) for i in range(devices)])
+        return lax.ppermute(block, "tok", [(i, i ^ s) for i in every])
 
     def columns(array, head):
         return lax.dynamic_slice_in_dim(array, head * size, size, 1)
@@ -116,8 +124,9 @@
     scaled_rows = (rates * clean_values.astype(f32)).astype(bf16)
     clean = []
     for s in range(heads):
-        piece = jnp.stack([columns(clean_keys, mine ^ s), columns(scaled_rows, mine ^ s)])
-        clean.append(piece if s == 0 else swap(piece, s))
+        other = clean_mine ^ s
+        piece = jnp.stack([columns(clean_keys, other), columns(scaled_rows, other)])
+        clean.append(piece if s == 0 else swap(piece, crossed(s)))
     keys = jnp.concatenate([p[0] for p in clean], axis=0)
     scaled = jnp.concatenate([p[1] for p in clean], axis=0)
 
@@ -128,11 +137,45 @@
         piece = own if s == 0 else swap(own, s)
         facts = lax.dynamic_update_slice(facts, piece, (mine ^ s, 0))
 
+    pieces = []
+    for s in range(heads):
+        piece = jnp.stack([columns(a, mine ^ s) for a in (noisy_tokens, swa_keys, swa_values)])
+        pieces.append(piece if s == 0 else swap(piece, s))
+    keys, scaled, pieces[1], pieces[2] = lax.optimization_barrier(
+        (keys, scaled, pieces[1], pieces[2])
+    )
+
+    def pick(h):
+        return [lax.dynamic_index_in_dim(w, h, 0, keepdims=False) for w in (w_in, w_gate, w_out)]
+
+    base = pick(clean_mine)
+    dot = functools.partial(lax.dot_general, preferred_element_type=f32)
+    nt, nn, tn = (((1,), (1,)), ((), ())), (((1,), (0,)), ((), ())), (((0,), (0,)), ((), ()))
+    first = dot(keys, base[0], nt)
+    second = dot(keys, base[1], nt)
+    sigmoid = jax.nn.sigmoid(first)
+    active = first * sigmoid
+    hidden = (active * second).astype(bf16)
+    d_act = dot(scaled, base[2], nn)
+    d_first = (d_act * second * sigmoid * (1.0 + first * (1.0 - sigmoid))).astype(bf16)
+    d_second = (d_act * active).astype(bf16)
+    d_first, d_second, hidden, pieces[3] = lax.optimization_barrier(
+        (d_first, d_second, hidden, pieces[3])
+    )
+    grads = jnp.concatenate(
+        [dot(d_first, keys, tn), dot(d_second, keys, tn), dot(scaled, hidden, tn)], axis=0
+    )
+    share = lax.psum_scatter(
+        grads, "tok", scatter_dimension=0, tiled=True, axis_index_groups=clean_peers
+    )
+    share = lax.ppermute(share.astype(bf16), "tok", [(i, crossed(i)) for i in every])
+    grad = lax.all_gather(
+        share, "tok", axis=0, tiled=True, axis_index_groups=peers
+    )
+
     noisy = jnp.zeros((3, rows, size), bf16)
     for s in range(heads):
-        piece = jnp.stack([columns(a, mine ^ s) for a in (noisy_tokens, swa_keys, swa_values)])
-        piece = piece if s == 0 else swap(piece, s)
-        noisy = lax.dynamic_update_slice(noisy, piece, (0, (mine ^ s) * count, 0))
+        noisy = lax.dynamic_update_slice(noisy, pieces[s], (0, (mine ^ s) * count, 0))
     z = noisy[0]
     kv = noisy[1:]
     earlier = []
@@ -144,31 +187,6 @@
         earlier.insert(0, carried)
     before = earlier[0] if len(earlier) == 1 else jnp.concatenate(earlier, axis=1)
 
-    base = [lax.dynamic_index_in_dim(w, mine, 0, keepdims=False) for w in (w_in, w_gate, w_out)]
-    dot = functools.partial(lax.dot_general, preferred_element_type=f32)
-    nt, nn, tn = (((1,), (1,)), ((), ())), (((1,), (0,)), ((), ())), (((0,), (0,)), ((), ()))
-    first = dot(keys, base[0], nt)
-    second = dot(keys, base[1], nt)
-    sigmoid = jax.nn.sigmoid(first)
-    active = first * sigmoid
-    hidden = (active * second).astype(bf16)
-    d_act = dot(scaled, base[2], nn)
-    d_first = (d_act * second * sigmoid * (1.0 + first * (1.0 - sigmoid))).astype(bf16)
-    d_second = (d_act * active).astype(bf16)
-    grads = jnp.concatenate(
-        [dot(d_first, keys, tn), dot(d_second, keys, tn), dot(scaled, hidden, tn)], axis=0
-    )
-    share = lax.psum_scatter(
-        grads, "tok", scatter_dimension=0, tiled=True, axis_index_groups=peers
-    )
-    grad = lax.all_gather(
-        share.astype(bf16), "tok", axis=0, tiled=True, axis_index_groups=peers
-    ).astype(f32)
-    own_power = jnp.broadcast_to(jnp.sum(grad * grad), (8, 128))
-    power = own_power
-    for s in range(1, heads):
-        power = power + swap(own_power, s)
-
     reach = facts[:, count + frames :].reshape(-1).astype(jnp.int32)
     first_token = (group * rows).astype(jnp.int32).reshape(1)
     half = size // SWDH // 2
@@ -179,9 +197,15 @@
         ],
         axis=1,
     )
+    grad, attended = lax.optimization_barrier((grad, attended))
+    grad = grad.astype(f32)
+    own_power = jnp.broadcast_to(jnp.sum(grad * grad), (8, 128))
+    power = own_power
+    for s in range(1, heads):
+        power = power + swap(own_power, s)
 
     grad_scale = lax.rsqrt(power[0, 0] / (3 * flat * size) + epsilon)
-    initial = jnp.concatenate(base, axis=0).astype(f32)
+    initial = jnp.concatenate(pick(mine), axis=0).astype(f32)
     update = initial + update_step * grad * grad_scale
     target = jnp.sqrt(jnp.mean(initial * initial, axis=-1, keepdims=True))
     memory = (

time: 248 us -> 261 us (1.052)
  waiting for transfers between devices: 121 us -> 137 us
  local copies, waits for them, and re-layouts: 36.7 us -> 31.7 us
    reduce_scatter x1, waiting for transfers between devices: 30.1 us -> 82.8 us  [local(): lax.psum_scatter(grads, 'tok', scatter_dimension=0, tiled=True, axis_inde...]
    ppermute x1, waiting for transfers between devices: 27.4 us -> 0.01 us  [local(): lax.ppermute(carried, 'tok', [(i, i + heads) for i in range(devices - hea...]
    ppermute x15 -> x16, waiting for transfers between devices: 59.8 us -> 36 us  [the longest x15 36 us: swap(): return lax.ppermute(block, 'tok', [(i, i ^ s) for i in every])]
    all_gather x1, waiting for transfers between devices: 3.53 us -> 18 us  [local(): lax.all_gather(share, 'tok', axis=0, tiled=True, axis_index_groups=peers)]
    unnamed x63 -> x41, local copies, waits for them, and re-layouts: 13.6 us -> 6.39 us
    ppermute x15 -> x16, starting transfers between devices: 10 us -> 11.3 us  [the longest x15 10.6 us: swap(): return lax.ppermute(block, 'tok', [(i, i ^ s) for i in every])]
  transfers between devices with their start and end apart: 18 -> 19, of which waited for: 9 -> 9; matrix products, arithmetic and copies ran while one was open for 10% -> 13% of each run, Pallas kernels for 10% -> 10%
where the time goes in v2:
time: 261 us; the launch traced here: 259 us
  waiting for transfers between devices  137 us (52%)
  local copies, waits for them, and re-layouts  31.7 us (12%)
  Pallas kernels  24.8 us (10%)
  other arithmetic  22 us (8%)
  starting transfers between devices  14.9 us (6%)
  between operations  14.7 us (6%)
  matrix products  14 us (5%)
    reduce_scatter x1, waiting for transfers between devices, local(): lax.psum_scatter(grads, 'tok', scatter_dimension=0, tiled=True, axis_inde...  82.8 us
    ppermute x15, waiting for transfers between devices, swap(): return lax.ppermute(block, 'tok', [(i, i ^ s) for i in every])  36 us
    pallas_call x2, Pallas kernels, attend(): pl.pallas_call(attend_kernel, out_shape=jax.ShapeDtypeStruct((rows, heads...  24.8 us
    all_gather x1, waiting for transfers between devices, local(): lax.all_gather(share, 'tok', axis=0, tiled=True, axis_index_groups=peers)  18 us
    ppermute x15, starting transfers between devices, swap(): return lax.ppermute(block, 'tok', [(i, i ^ s) for i in every])  10.6 us
    unnamed x41, local copies, waits for them, and re-layouts  6.39 us
  transfers between devices with their start and end apart: 19, of which 9 were waited for; matrix products, arithmetic and copies ran while one was open for 13% of the time, Pallas kernels for 10%

profile of v2, /device:TPU:8, one launch (start us, length us, event | category | flops | bytes accessed | tf_op | source)
XLA Modules:
  0.0 259.0 jit_solution(2842559063642809945)
XLA Ops:
  6.5 1.0 copy.16
  7.9 0.9 copy.18
  9.4 2.2 constant_dynamic-slice_fusion.5
  12.4 1.0 collective-permute-start.2
  16.0 2.5 dynamic-slice_bitcast_fusion.18
  18.7 1.0 pad_maximum_fusion.5
  19.8 1.0 pad_maximum_fusion.6
  20.8 1.5 collective-permute-start.4
  22.3 1.0 pad_maximum_fusion.7
  23.3 3.6 %collective-permute-done.2 = bf16[2,256,512]{2,1,0:T(8,128)(2,1)} collective-permute-done((bf16[2,256,512]{2,1,0:T(8,128)(2,1)}, bf16[2,256,512]{2,1,0:T(8,128)(2,1)}, u32[]{:S(2)}, u32[]{:S(2)}) %collective-permute-start.2) | collective-permute-done | bytes 524320 | tf_op jit(solution)/shard_map/ppermute | solution.py:118
  26.9 1.4 collective-permute-start.5
  28.3 1.1 slice_bitcast_fusion.5
  29.3 8.9 %collective-permute-done.1 = bf16[2,256,512]{2,1,0:T(8,128)(2,1)} collective-permute-done((bf16[2,256,512]{2,1,0:T(8,128)(2,1)}, bf16[2,256,512]{2,1,0:T(8,128)(2,1)}, u32[]{:S(2)}, u32[]{:S(2)}) %collective-permute-start.1) | collective-permute-done | bytes 524320 | tf_op jit(solution)/shard_map/ppermute | solution.py:118
  38.2 1.1 slice_bitcast_fusion.6
  39.3 1.1 slice_bitcast_fusion.7
  40.5 0.9 collective-permute-done.4
  42.2 1.8 fusion.15
  44.0 2.6 %multiply_convert_fusion.2 = (bf16[1024,512]{1,0:T(8,128)(2,1)S(1)}, bf16[1024,512]{1,0:T(8,128)(2,1)S(1)}, bf16[1024,512]{1,0:T(8,128)(2,1)S(1)}) fusion(f32[1024,512]{1,0:T(8,128)S(1)} %fusion.11, f32[1024,512]{1,0:T(8,128)S(1)} %fusion.15, bf16[1024,512]{1,0:T(8,128)(2,1)S(1)} %pad_maximum_fusion.3, bf16[4,512,512]{2,1,0:T(8,128)(2,1)} %param.19, ...), kind=kOutput, calls=%fused_computation.19 | convolution fusion | flops 544735232 | bytes 8912900 | tf_op jit(solution)/shard_map/dot_general | solution.py:155
  46.6 10.4 %collective-permute-done.5 = bf16[3,256,512]{2,1,0:T(8,128)(2,1)S(1)} collective-permute-done((bf16[3,256,512]{2,1,0:T(8,128)(2,1)}, bf16[3,256,512]{2,1,0:T(8,128)(2,1)S(1)}, u32[]{:S(2)}, u32[]{:S(2)}) %collective-permute-start.5) | collective-permute-done | bytes 786464 | tf_op jit(solution)/shard_map/ppermute | solution.py:118
  57.1 0.9 copy-done.13
  60.1 2.0 pad_maximum_fusion
  63.6 1.5 collective-permute-start.7
  65.5 1.3 constant_dynamic-update-slice_fusion.5
  66.8 1.2 constant_dynamic-update-slice_fusion.4
  68.1 1.5 slice.104
  70.4 3.5 %collective-permute-start.10 = (bf16[2,1024,512]{2,1,0:T(8,128)(2,1)}, bf16[2,1024,512]{2,1,0:T(8,128)(2,1)}, u32[]{:S(2)}, u32[]{:S(2)}) collective-permute-start(bf16[2,1024,512]{2,1,0:T(8,128)(2,1)} %slice.104), channel_id=1, source_target_pairs={{0,4},{1,5},{2,6},{3,7},{4,8},{5,9},{6,10},{7,11},{8,12},{9,13},{1... | collective-permute-start | bytes 6291464 | tf_op jit(solution)/shard_map/ppermute | solution.py:184
  73.9 82.8 %reduce-scatter.2.cloned.1.call-done = f32[192,512]{1,0:T(8,128)} async-done(((f32[1536,512]{1,0:T(8,128)}), f32[192,512]{1,0:T(8,128)}) %reduce-scatter.2.cloned.1.call-update) | async-done | bytes 393232 | tf_op jit(solution)/shard_map/reduce_scatter | solution.py:168
  156.7 1.0 convert_element_type.75
  158.5 1.3 dynamic-slice_bitcast_fusion
  163.1 2.1 slice_bitcast_fusion
  165.2 1.7 slice_bitcast_fusion.1
  166.9 12.5 %shard_map.128 = f32[1024,256]{1,0:T(8,128)S(1)} custom-call(s32[8]{0:T(128)S(1)} %convert_element_type.77.reach_ref, s32[1]{0:T(128)} %bitcast.33.first_ref, bf16[1024,512]{1,0:T(8,128)(2,1)S(1)} %get-tuple-element.33.q_ref, bf16[1024,512]{1,0:T(8,128)(2,1)S(1)} %get-tuple-element.35.kp_ref, bf16[1024,512]{1,0:T(8,128)(2,1)S(1)} %get-tuple-element.32.kc_ref, ...), custom_call_target="tpu_custom_call" | custom-call | flops 4831838208 | bytes 4194304 | tf_op jit(solution)/shard_map/pallas_call | solution.py:54
  179.4 12.3 %shard_map.127 = f32[1024,256]{1,0:T(8,128)S(1)} custom-call(s32[8]{0:T(128)S(1)} %convert_element_type.77.reach_ref, s32[1]{0:T(128)} %bitcast.33.first_ref, bf16[1024,512]{1,0:T(8,128)(2,1)S(1)} %get-tuple-element.33.q_ref, bf16[1024,512]{1,0:T(8,128)(2,1)S(1)} %get-tuple-element.35.kp_ref, bf16[1024,512]{1,0:T(8,128)(2,1)S(1)} %get-tuple-element.32.kc_ref, ...), custom_call_target="tpu_custom_call" | custom-call | flops 4831838208 | bytes 4194304 | tf_op jit(solution)/shard_map/pallas_call | solution.py:54
  191.7 1.6 pad_maximum_fusion.1
  193.3 18.0 %all-gather.2.cloned.1.call-done = bf16[1536,512]{1,0:T(8,128)(2,1)} async-done(((bf16[192,512]{1,0:T(8,128)(2,1)}), bf16[1536,512]{1,0:T(8,128)(2,1)}) %all-gather.2.cloned.1.call-update) | async-done | bytes 1572880 | tf_op jit(solution)/shard_map/all_gather | solution.py:172
  211.3 2.9 %fusion.1 = f32[]{:T(128)} fusion(bf16[1536,512]{1,0:T(8,128)(2,1)} %all-gather.2.cloned.1.call-done), kind=kLoop, calls=%fused_computation.7 | loop fusion | flops 2359295 | bytes 1572868 | tf_op jit(solution)/shard_map/reduce_sum | solution.py:202
  215.2 1.3 collective-permute-start.12
  216.8 1.6 fusion.2
  220.7 1.0 fusion
  221.7 2.8 %multiply_convert_fusion = bf16[1536,512]{1,0:T(8,128)(2,1)S(1)} fusion(bf16[1536,512]{1,0:T(8,128)(2,1)S(1)} %copy-done.3, f32[1536]{0:T(1024)S(1)} %add_rsqrt_fusion, f32[1536]{0:T(1024)S(1)} %multiply_sqrt_fusion, f32[]{:T(128)} %bitcast.38, bf16[512,512]{1,0:T(8,128)(2,1)S(1)} %get-tuple-element.84, bf16[512,512]{1,0:T(8,128)(2,1)S(1)} %get-tuple-element.85, ...), kind=kLoop, calls=%fused_computation.9 | loop fusion | flops 9437184 | bytes 4730884 | tf_op jit(solution)/shard_map/convert_element_type | solution.py:213
  224.5 1.2 copy-done.6
  225.7 2.1 fusion.9
  227.8 4.6 %multiply_reduce_fusion.1 = (f32[1024]{0:T(1024)S(1)}, f32[1024,512]{0,1:T(8,128)}) fusion(bf16[1536,512]{1,0:T(8,128)(2,1)} %copy-done.6, f32[1024,512]{1,0:T(8,128)} %fusion.9, bf16[1024,512]{1,0:T(8,128)(2,1)S(1)} %fusion.2), kind=kOutput, calls=%fused_computation.16 | convolution fusion | flops 1077935104 | bytes 6295552 | tf_op jit(solution)/shard_map/dot_general | solution.py:226
  232.4 3.0 %copy.17 = f32[1024,512]{1,0:T(8,128)} copy(f32[1024,512]{0,1:T(8,128)} %get-tuple-element.73) | data formatting | bytes 4194304 | tf_op jit(solution)/shard_map/dot_general | solution.py:226
  235.5 1.9 add_convert_fusion
  237.9 1.2 collective-permute-start.15
  239.6 7.4 %collective-permute-done.15 = bf16[256,512]{1,0:T(8,128)(2,1)S(1)} collective-permute-done((bf16[256,512]{1,0:T(8,128)(2,1)S(1)}, bf16[256,512]{1,0:T(8,128)(2,1)S(1)}, u32[]{:S(2)}, u32[]{:S(2)}) %collective-permute-start.15) | collective-permute-done | bytes 262176 | tf_op jit(solution)/shard_map/ppermute | solution.py:118
  247.0 4.4 %collective-permute-done.16 = bf16[256,512]{1,0:T(8,128)(2,1)S(1)} collective-permute-done((bf16[256,512]{1,0:T(8,128)(2,1)S(1)}, bf16[256,512]{1,0:T(8,128)(2,1)S(1)}, u32[]{:S(2)}, u32[]{:S(2)}) %collective-permute-start.16) | collective-permute-done | bytes 262176 | tf_op jit(solution)/shard_map/ppermute | solution.py:118
  (113 shorter events, 19.0 us)
Async XLA Ops:
  6.5 34.9 %copy-start = (bf16[4,512,512]{2,1,0:T(8,128)(2,1)S(1)}, bf16[4,512,512]{2,1,0:T(8,128)(2,1)}, u32[]{:S(2)}) copy-start(bf16[4,512,512]{2,1,0:T(8,128)(2,1)} %param.18) | copy-start | bytes 6291460
  6.5 150.2 %reduce-scatter.2.cloned.1.call-start = ((), (), s32[]{:S(2)}) async-start(), calls=%async_computation.1 | async-start | bytes 3538944 | tf_op jit(solution)/shard_map/reduce_scatter | solution.py:168
  7.9 1.2 copy-start.8
  12.4 14.5 %collective-permute-start.2 = (bf16[2,256,512]{2,1,0:T(8,128)(2,1)}, bf16[2,256,512]{2,1,0:T(8,128)(2,1)}, u32[]{:S(2)}, u32[]{:S(2)}) collective-permute-start(bf16[2,256,512]{2,1,0:T(8,128)(2,1)} %pad_maximum_fusion.10), channel_id=1, source_target_pairs={{0,5},{1,4},{2,7},{3,6},{4,1},{5,0},{6,3},{7,2},{8,13},{9,12},{10,... | collective-permute-start | bytes 1572872 | tf_op jit(solution)/shard_map/ppermute | solution.py:118
  14.2 24.0 %collective-permute-start.1 = (bf16[2,256,512]{2,1,0:T(8,128)(2,1)}, bf16[2,256,512]{2,1,0:T(8,128)(2,1)}, u32[]{:S(2)}, u32[]{:S(2)}) collective-permute-start(bf16[2,256,512]{2,1,0:T(8,128)(2,1)} %pad_maximum_fusion.9), channel_id=1, source_target_pairs={{0,4},{1,5},{2,6},{3,7},{4,0},{5,1},{6,2},{7,3},{8,12},{9,13},{10,... | collective-permute-start | bytes 1572872 | tf_op jit(solution)/shard_map/ppermute | solution.py:118
  15.7 23.6 %collective-permute-start = (bf16[2,256,512]{2,1,0:T(8,128)(2,1)}, bf16[2,256,512]{2,1,0:T(8,128)(2,1)}, u32[]{:S(2)}, u32[]{:S(2)}) collective-permute-start(bf16[2,256,512]{2,1,0:T(8,128)(2,1)} %pad_maximum_fusion.8), channel_id=1, source_target_pairs={{0,1},{1,0},{2,3},{3,2},{4,5},{5,4},{6,7},{7,6},{8,9},{9,8},{10,11... | collective-permute-start | bytes 1572872 | tf_op jit(solution)/shard_map/ppermute | solution.py:118
  16.0 2.5 copy-start.5
  19.6 20.9 %collective-permute-start.3 = (bf16[3,256,512]{2,1,0:T(8,128)(2,1)}, bf16[3,256,512]{2,1,0:T(8,128)(2,1)}, u32[]{:S(2)}, u32[]{:S(2)}) collective-permute-start(bf16[3,256,512]{2,1,0:T(8,128)(2,1)} %pad_maximum_fusion.5), channel_id=1, source_target_pairs={{0,1},{1,0},{2,3},{3,2},{4,5},{5,4},{6,7},{7,6},{8,9},{9,8},{10,11... | collective-permute-start | bytes 2359304 | tf_op jit(solution)/shard_map/ppermute | solution.py:118
  20.8 20.7 %collective-permute-start.4 = (bf16[3,256,512]{2,1,0:T(8,128)(2,1)}, bf16[3,256,512]{2,1,0:T(8,128)(2,1)}, u32[]{:S(2)}, u32[]{:S(2)}) collective-permute-start(bf16[3,256,512]{2,1,0:T(8,128)(2,1)} %pad_maximum_fusion.6), channel_id=1, source_target_pairs={{0,2},{1,3},{2,0},{3,1},{4,6},{5,7},{6,4},{7,5},{8,10},{9,11},{10,... | collective-permute-start | bytes 2359304 | tf_op jit(solution)/shard_map/ppermute | solution.py:118
  23.3 17.1 %copy-start.12 = (bf16[256,512]{1,0:T(8,128)(2,1)S(1)}, bf16[256,512]{1,0:T(8,128)(2,1)}, u32[]{:S(2)}) copy-start(bf16[256,512]{1,0:T(8,128)(2,1)} %get-tuple-element.77) | copy-start | bytes 786436
  26.9 30.2 %collective-permute-start.5 = (bf16[3,256,512]{2,1,0:T(8,128)(2,1)}, bf16[3,256,512]{2,1,0:T(8,128)(2,1)S(1)}, u32[]{:S(2)}, u32[]{:S(2)}) collective-permute-start(bf16[3,256,512]{2,1,0:T(8,128)(2,1)} %pad_maximum_fusion.7), channel_id=1, source_target_pairs={{0,3},{1,2},{2,1},{3,0},{4,7},{5,6},{6,5},{7,4},{8,11},{9,10},{10,... | collective-permute-start | bytes 2359304 | tf_op jit(solution)/shard_map/ppermute | solution.py:118
  29.3 11.1 %copy-start.11 = (bf16[256,512]{1,0:T(8,128)(2,1)S(1)}, bf16[256,512]{1,0:T(8,128)(2,1)}, u32[]{:S(2)}) copy-start(bf16[256,512]{1,0:T(8,128)(2,1)} %get-tuple-element.52) | copy-start | bytes 786436
  57.1 0.9 copy-start.13
  62.1 0.7 copy-start.17
  62.1 0.7 copy-start.18
  62.2 149.1 %all-gather.2.cloned.1.call-start = ((), (), s32[]{:S(2)}) async-start(), calls=%async_computation.2 | async-start | bytes 1769472 | tf_op jit(solution)/shard_map/all_gather | solution.py:172
  63.1 2.3 copy-start.9
  63.1 2.3 copy-start.10
  63.2 98.1 %collective-permute-start.6 = (f32[1,260]{1,0:T(1,128)S(1)}, f32[1,260]{1,0:T(1,128)S(1)}, u32[]{:S(2)}, u32[]{:S(2)}) collective-permute-start(f32[1,260]{1,0:T(1,128)S(1)} %broadcast_in_dim.37), channel_id=1, source_target_pairs={{0,1},{1,0},{2,3},{3,2},{4,5},{5,4},{6,7},{7,6},{8,9},{9,8},{10,11... | collective-permute-start | bytes 3128 | tf_op jit(solution)/shard_map/ppermute | solution.py:118
  63.6 97.7 %collective-permute-start.7 = (f32[1,260]{1,0:T(1,128)S(1)}, f32[1,260]{1,0:T(1,128)S(1)}, u32[]{:S(2)}, u32[]{:S(2)}) collective-permute-start(f32[1,260]{1,0:T(1,128)S(1)} %broadcast_in_dim.37), channel_id=1, source_target_pairs={{0,2},{1,3},{2,0},{3,1},{4,6},{5,7},{6,4},{7,5},{8,10},{9,11},{10,... | collective-permute-start | bytes 3128 | tf_op jit(solution)/shard_map/ppermute | solution.py:118
  65.1 96.3 %collective-permute-start.8 = (f32[1,260]{1,0:T(1,128)S(1)}, f32[1,260]{1,0:T(1,128)S(1)}, u32[]{:S(2)}, u32[]{:S(2)}) collective-permute-start(f32[1,260]{1,0:T(1,128)S(1)} %broadcast_in_dim.37), channel_id=1, source_target_pairs={{0,3},{1,2},{2,1},{3,0},{4,7},{5,6},{6,5},{7,4},{8,11},{9,10},{10,... | collective-permute-start | bytes 3128 | tf_op jit(solution)/shard_map/ppermute | solution.py:118
  65.4 2.6 copy-start.14
  68.1 2.3 copy-start.2
  68.1 5.8 %copy-start.16 = (f32[8,4096]{1,0:T(8,128)S(1)}, f32[8,4096]{1,0:T(8,128)}, u32[]{:S(2)}) copy-start(f32[8,4096]{1,0:T(8,128)} %param.26) | copy-start | bytes 393220
  70.4 94.8 %collective-permute-start.10 = (bf16[2,1024,512]{2,1,0:T(8,128)(2,1)}, bf16[2,1024,512]{2,1,0:T(8,128)(2,1)}, u32[]{:S(2)}, u32[]{:S(2)}) collective-permute-start(bf16[2,1024,512]{2,1,0:T(8,128)(2,1)} %slice.104), channel_id=1, source_target_pairs={{0,4},{1,5},{2,6},{3,7},{4,8},{5,9},{6,10},{7,11},{8,12},{9,13},{1... | collective-permute-start | bytes 6291464 | tf_op jit(solution)/shard_map/ppermute | solution.py:184
  157.7 2.0 collective-permute-start.9
  159.7 0.7 copy-start.15
  211.3 9.4 %copy-start.3 = (bf16[1536,512]{1,0:T(8,128)(2,1)S(1)}, bf16[1536,512]{1,0:T(8,128)(2,1)}, u32[]{:S(2)}) copy-start(bf16[1536,512]{1,0:T(8,128)(2,1)} %all-gather.2.cloned.1.call-done) | copy-start | bytes 4718596
  214.9 3.5 %collective-permute-start.13 = (f32[8,128]{1,0:T(8,128)S(1)}, f32[8,128]{1,0:T(8,128)S(1)}, u32[]{:S(2)}, u32[]{:S(2)}) collective-permute-start(f32[8,128]{1,0:T(8,128)S(1)} %broadcast_in_dim.38), channel_id=1, source_target_pairs={{0,3},{1,2},{2,1},{3,0},{4,7},{5,6},{6,5},{7,4},{8,11},{9,10},{10,... | collective-permute-start | bytes 12296 | tf_op jit(solution)/shard_map/ppermute | solution.py:118
  215.2 3.6 %collective-permute-start.12 = (f32[8,128]{1,0:T(8,128)S(1)}, f32[8,128]{1,0:T(8,128)S(1)}, u32[]{:S(2)}, u32[]{:S(2)}) collective-permute-start(f32[8,128]{1,0:T(8,128)S(1)} %broadcast_in_dim.38), channel_id=1, source_target_pairs={{0,2},{1,3},{2,0},{3,1},{4,6},{5,7},{6,4},{7,5},{8,10},{9,11},{10,... | collective-permute-start | bytes 12296 | tf_op jit(solution)/shard_map/ppermute | solution.py:118
  216.5 2.3 collective-permute-start.11
  224.5 1.2 copy-start.6
  232.4 3.0 %copy-start.4 = (f32[1024,512]{1,0:T(8,128)S(1)}, f32[1024,512]{1,0:T(8,128)}, u32[]{:S(2)}) copy-start(f32[1024,512]{1,0:T(8,128)} %pad_maximum_fusion.1) | copy-start | bytes 6291460
  237.4 14.8 %copy-start.1 = (bf16[4,512,512]{2,1,0:T(8,128)(2,1)S(1)}, bf16[4,512,512]{2,1,0:T(8,128)(2,1)}, u32[]{:S(2)}) copy-start(bf16[4,512,512]{2,1,0:T(8,128)(2,1)} %param.18) | copy-start | bytes 6291460
  237.6 1.9 collective-permute-start.14
  237.9 9.1 %collective-permute-start.15 = (bf16[256,512]{1,0:T(8,128)(2,1)S(1)}, bf16[256,512]{1,0:T(8,128)(2,1)S(1)}, u32[]{:S(2)}, u32[]{:S(2)}) collective-permute-start(bf16[256,512]{1,0:T(8,128)(2,1)S(1)} %get-tuple-element.37), channel_id=1, source_target_pairs={{0,2},{1,3},{2,0},{3,1},{4,6},{5,7},{6,4},{7,5},{8,10},{9,11},{10,... | collective-permute-start | bytes 786440 | tf_op jit(solution)/shard_map/ppermute | solution.py:118
  239.1 12.3 %collective-permute-start.16 = (bf16[256,512]{1,0:T(8,128)(2,1)S(1)}, bf16[256,512]{1,0:T(8,128)(2,1)S(1)}, u32[]{:S(2)}, u32[]{:S(2)}) collective-permute-start(bf16[256,512]{1,0:T(8,128)(2,1)S(1)} %get-tuple-element.36), channel_id=1, source_target_pairs={{0,3},{1,2},{2,1},{3,0},{4,7},{5,6},{6,5},{7,4},{8,11},{9,10},{10,... | collective-permute-start | bytes 786440 | tf_op jit(solution)/shard_map/ppermute | solution.py:118
  247.0 4.4 %copy-start.7 = (bf16[256,2048]{1,0:T(8,128)(2,1)}, bf16[256,2048]{1,0:T(8,128)(2,1)S(1)}, u32[]{:S(2)}) copy-start(bf16[256,2048]{1,0:T(8,128)(2,1)S(1)} %constant_dynamic-update-slice_fusion.1) | copy-start | bytes 3145732
Sparse Core Ops, SparseCore 0:
  62.3 94.3 reduce-scatter.1
  160.6 50.6 all-gather.1

commit v3 on v2

--- a/solution.py
+++ b/solution.py
@@ -165,9 +165,15 @@
     grads = jnp.concatenate(
         [dot(d_first, keys, tn), dot(d_second, keys, tn), dot(scaled, hidden, tn)], axis=0
     )
-    share = lax.psum_scatter(
-        grads, "tok", scatter_dimension=0, tiled=True, axis_index_groups=clean_peers
-    )
+    fellows = len(clean_peers[0])
+    ranks = {i: r for row in clean_peers for r, i in enumerate(row)}
+    rank = jnp.array([ranks[i] for i in every], jnp.int32)[position]
+    depth = grads.shape[0] // fellows
+    share = lax.dynamic_slice_in_dim(grads, rank * depth, depth, 0)
+    for s in range(1, fellows):
+        route = [(row[r], row[(r + s) % fellows]) for row in clean_peers for r in range(fellows)]
+        block = lax.dynamic_slice_in_dim(grads, (rank + s) % fellows * depth, depth, 0)
+        share = share + lax.ppermute(block, "tok", route)
     share = lax.ppermute(share.astype(bf16), "tok", [(i, crossed(i)) for i in every])
     grad = lax.all_gather(
         share, "tok", axis=0, tiled=True, axis_index_groups=peers

time: 261 us -> 281 us (1.077)
  the two profiles are of different devices: /device:TPU:8 before, /device:TPU:17 now
where the time goes in v3:
time: 281 us
  waiting for transfers between devices  133 us (47%)
  local copies, waits for them, and re-layouts  38.7 us (14%)
  starting transfers between devices  27 us (10%)
  Pallas kernels  24.8 us (9%)
  other arithmetic  22.6 us (8%)
  between operations  20.3 us (7%)
  matrix products  14.1 us (5%)
    ppermute x1, waiting for transfers between devices, local(): lax.ppermute(carried, 'tok', [(i, i + heads) for i in range(devices - hea...  54 us
    ppermute x7, waiting for transfers between devices, local(): share = share + lax.ppermute(block, 'tok', route)  51.8 us
    ppermute x15, waiting for transfers between devices, swap(): return lax.ppermute(block, 'tok', [(i, i ^ s) for i in every])  27.3 us
    pallas_call x2, Pallas kernels, attend(): pl.pallas_call(attend_kernel, out_shape=jax.ShapeDtypeStruct((rows, heads...  24.8 us
    ppermute x15, starting transfers between devices, swap(): return lax.ppermute(block, 'tok', [(i, i ^ s) for i in every])  15 us
    ppermute x7, starting transfers between devices, local(): share = share + lax.ppermute(block, 'tok', route)  8.22 us
    unnamed x49, local copies, waits for them, and re-layouts  5.93 us
  transfers between devices with their start and end apart: 25, of which 12 were waited for; matrix products, arithmetic and copies ran while one was open for 14% of the time, Pallas kernels for 9%

profile of v3, /device:TPU:17, one launch (start us, length us, event | category | flops | bytes accessed | tf_op | source)
XLA Modules:
  0.0 280.6 jit_solution(8593062066028947888)
XLA Ops:
  9.4 2.2 constant_dynamic-slice_fusion.12
  12.4 1.8 collective-permute-start.2
  18.0 1.1 dynamic-slice_bitcast_fusion.18
  21.4 1.2 collective-permute-start.4
  22.9 1.3 pad_maximum_fusion.7
  24.2 1.9 broadcast_in_dim.34
  34.1 1.1 slice_bitcast_fusion.5
  35.2 3.2 %collective-permute-done.1 = bf16[2,256,512]{2,1,0:T(8,128)(2,1)} collective-permute-done((bf16[2,256,512]{2,1,0:T(8,128)(2,1)}, bf16[2,256,512]{2,1,0:T(8,128)(2,1)}, u32[]{:S(2)}, u32[]{:S(2)}) %collective-permute-start.1) | collective-permute-done | bytes 524320 | tf_op jit(solution)/shard_map/ppermute | solution.py:118
  38.4 1.1 slice_bitcast_fusion.6
  39.5 1.1 slice_bitcast_fusion.7
  41.5 1.7 fusion.15
  43.3 2.6 multiply_convert_fusion.2
  45.9 11.8 %collective-permute-done.5 = bf16[3,256,512]{2,1,0:T(8,128)(2,1)S(1)} collective-permute-done((bf16[3,256,512]{2,1,0:T(8,128)(2,1)S(1)}, bf16[3,256,512]{2,1,0:T(8,128)(2,1)S(1)}, u32[]{:S(2)}, u32[]{:S(2)}) %collective-permute-start.5) | collective-permute-done | bytes 786464 | tf_op jit(solution)/shard_map/ppermute | solution.py:118
  60.3 1.5 constant_dynamic-slice_fusion.9
  62.0 1.1 collective-permute-start.15
  63.3 3.4 %collective-permute-start.13 = (f32[192,512]{1,0:T(8,128)S(1)}, f32[192,512]{1,0:T(8,128)S(1)}, u32[]{:S(2)}, u32[]{:S(2)}) collective-permute-start(f32[192,512]{1,0:T(8,128)S(1)} %get-tuple-element.37), channel_id=1, source_target_pairs={{0,18},{2,24},{8,26},{10,0},{16,2},{18,8},{24,10},{26,16},{1,19},{... | collective-permute-start | bytes 1179656 | tf_op jit(solution)/shard_map/ppermute | solution.py:176
  66.7 2.3 collective-permute-start.11
  68.9 3.8 %collective-permute-done.15 = f32[192,512]{1,0:T(8,128)S(1)} collective-permute-done((f32[192,512]{1,0:T(8,128)S(1)}, f32[192,512]{1,0:T(8,128)S(1)}, u32[]{:S(2)}, u32[]{:S(2)}) %collective-permute-start.15) | collective-permute-done | bytes 393248 | tf_op jit(solution)/shard_map/ppermute | solution.py:176
  72.7 1.3 collective-permute-start.10
  74.0 8.0 %collective-permute-done.14 = f32[192,512]{1,0:T(8,128)S(1)} collective-permute-done((f32[192,512]{1,0:T(8,128)S(1)}, f32[192,512]{1,0:T(8,128)S(1)}, u32[]{:S(2)}, u32[]{:S(2)}) %collective-permute-start.14) | collective-permute-done | bytes 393248 | tf_op jit(solution)/shard_map/ppermute | solution.py:176
  82.1 2.2 constant_dynamic-update-slice_fusion.5
  84.3 2.1 constant_dynamic-update-slice_fusion.4
  87.3 3.1 %slice.104 = bf16[2,1024,512]{2,1,0:T(8,128)(2,1)} slice(bf16[3,1024,512]{2,1,0:T(8,128)(2,1)} %constant_dynamic-update-slice_fusion.3), slice={[1:3], [0:1024], [0:512]} | slice | bytes 4194304 | tf_op jit(solution)/shard_map/slice | solution.py:186
  90.4 31.6 %collective-permute-done.13 = f32[192,512]{1,0:T(8,128)S(1)} collective-permute-done((f32[192,512]{1,0:T(8,128)S(1)}, f32[192,512]{1,0:T(8,128)S(1)}, u32[]{:S(2)}, u32[]{:S(2)}) %collective-permute-start.13) | collective-permute-done | bytes 393248 | tf_op jit(solution)/shard_map/ppermute | solution.py:176
  122.8 3.1 %collective-permute-start.17 = (bf16[2,1024,512]{2,1,0:T(8,128)(2,1)}, bf16[2,1024,512]{2,1,0:T(8,128)(2,1)}, u32[]{:S(2)}, u32[]{:S(2)}) collective-permute-start(bf16[2,1024,512]{2,1,0:T(8,128)(2,1)} %slice.104), channel_id=1, source_target_pairs={{0,4},{1,5},{2,6},{3,7},{4,8},{5,9},{6,10},{7,11},{8,12},{9,13},{1... | collective-permute-start | bytes 6291464 | tf_op jit(solution)/shard_map/ppermute | solution.py:190
  125.9 4.6 %collective-permute-done.12 = f32[192,512]{1,0:T(8,128)} collective-permute-done((f32[192,512]{1,0:T(8,128)}, f32[192,512]{1,0:T(8,128)}, u32[]{:S(2)}, u32[]{:S(2)}) %collective-permute-start.12) | collective-permute-done | bytes 393248 | tf_op jit(solution)/shard_map/ppermute | solution.py:176
  131.5 3.5 %collective-permute-done.10 = f32[192,512]{1,0:T(8,128)} collective-permute-done((f32[192,512]{1,0:T(8,128)S(1)}, f32[192,512]{1,0:T(8,128)}, u32[]{:S(2)}, u32[]{:S(2)}) %collective-permute-start.10) | collective-permute-done | bytes 393248 | tf_op jit(solution)/shard_map/ppermute | solution.py:176
  135.3 2.1 add_convert_fusion.1
  138.2 1.3 dynamic-slice_bitcast_fusion
  142.8 2.1 slice_bitcast_fusion
  144.9 54.0 %collective-permute-done.17 = bf16[2,1024,512]{2,1,0:T(8,128)(2,1)} collective-permute-done((bf16[2,1024,512]{2,1,0:T(8,128)(2,1)}, bf16[2,1024,512]{2,1,0:T(8,128)(2,1)}, u32[]{:S(2)}, u32[]{:S(2)}) %collective-permute-start.17) | collective-permute-done | bytes 2097184 | tf_op jit(solution)/shard_map/ppermute | solution.py:190
  198.9 1.7 slice_bitcast_fusion.1
  200.6 12.5 %shard_map.137 = f32[1024,256]{1,0:T(8,128)S(1)} custom-call(s32[8]{0:T(128)S(1)} %convert_element_type.77.reach_ref, s32[1]{0:T(128)} %bitcast.41.first_ref, bf16[1024,512]{1,0:T(8,128)(2,1)S(1)} %get-tuple-element.33.q_ref, bf16[1024,512]{1,0:T(8,128)(2,1)S(1)} %get-tuple-element.42.kp_ref, bf16[1024,512]{1,0:T(8,128)(2,1)S(1)} %get-tuple-element.32.kc_ref, ...), custom_call_target="tpu_custom_call" | custom-call | flops 4831838208 | bytes 4194304 | tf_op jit(solution)/shard_map/pallas_call | solution.py:54
  213.0 12.3 %shard_map.136 = f32[1024,256]{1,0:T(8,128)S(1)} custom-call(s32[8]{0:T(128)S(1)} %convert_element_type.77.reach_ref, s32[1]{0:T(128)} %bitcast.41.first_ref, bf16[1024,512]{1,0:T(8,128)(2,1)S(1)} %get-tuple-element.33.q_ref, bf16[1024,512]{1,0:T(8,128)(2,1)S(1)} %get-tuple-element.42.kp_ref, bf16[1024,512]{1,0:T(8,128)(2,1)S(1)} %get-tuple-element.32.kc_ref, ...), custom_call_target="tpu_custom_call" | custom-call | flops 4831838208 | bytes 4194304 | tf_op jit(solution)/shard_map/pallas_call | solution.py:54
  225.4 1.6 pad_maximum_fusion.1
  227.0 2.9 %fusion.1 = f32[]{:T(128)} fusion(bf16[1536,512]{1,0:T(8,128)(2,1)} %all-gather.2.cloned.1.call-done), kind=kLoop, calls=%fused_computation.7 | loop fusion | flops 2359295 | bytes 1572868 | tf_op jit(solution)/shard_map/reduce_sum | solution.py:208
  230.6 6.2 %collective-permute-start.20 = (f32[8,128]{1,0:T(8,128)S(1)}, f32[8,128]{1,0:T(8,128)S(1)}, u32[]{:S(2)}, u32[]{:S(2)}) collective-permute-start(f32[8,128]{1,0:T(8,128)S(1)} %broadcast_in_dim.38), channel_id=1, source_target_pairs={{0,3},{1,2},{2,1},{3,0},{4,7},{5,6},{6,5},{7,4},{8,11},{9,10},{10,... | collective-permute-start | bytes 12296 | tf_op jit(solution)/shard_map/ppermute | solution.py:118
  237.3 1.6 fusion.2
  242.1 2.8 %multiply_convert_fusion = bf16[1536,512]{1,0:T(8,128)(2,1)S(1)} fusion(bf16[1536,512]{1,0:T(8,128)(2,1)S(1)} %copy-done.2, f32[1536]{0:T(1024)S(1)} %add_rsqrt_fusion, f32[1536]{0:T(1024)S(1)} %multiply_sqrt_fusion, f32[]{:T(128)} %bitcast.46, bf16[512,512]{1,0:T(8,128)(2,1)S(1)} %get-tuple-element.91, bf16[512,512]{1,0:T(8,128)(2,1)S(1)} %get-tuple-element.92, ...), kind=kLoop, calls=%fused_computation.9 | loop fusion | flops 9437184 | bytes 4730884 | tf_op jit(solution)/shard_map/convert_element_type | solution.py:219
  244.9 1.2 copy-done.6
  246.1 2.1 fusion.9
  248.2 4.6 %multiply_reduce_fusion.1 = (f32[1024]{0:T(1024)S(1)}, f32[1024,512]{0,1:T(8,128)}) fusion(bf16[1536,512]{1,0:T(8,128)(2,1)} %copy-done.6, f32[1024,512]{1,0:T(8,128)} %fusion.9, bf16[1024,512]{1,0:T(8,128)(2,1)S(1)} %fusion.2), kind=kOutput, calls=%fused_computation.16 | convolution fusion | flops 1077935104 | bytes 6295552 | tf_op jit(solution)/shard_map/dot_general | solution.py:232
  252.9 3.1 %copy.18 = f32[1024,512]{1,0:T(8,128)} copy(f32[1024,512]{0,1:T(8,128)} %get-tuple-element.80) | data formatting | bytes 4194304 | tf_op jit(solution)/shard_map/dot_general | solution.py:232
  255.9 1.9 add_convert_fusion
  258.1 1.2 collective-permute-start.21
  259.5 1.5 collective-permute-start.23
  261.1 6.1 %collective-permute-done.22 = bf16[256,512]{1,0:T(8,128)(2,1)S(1)} collective-permute-done((bf16[256,512]{1,0:T(8,128)(2,1)S(1)}, bf16[256,512]{1,0:T(8,128)(2,1)S(1)}, u32[]{:S(2)}, u32[]{:S(2)}) %collective-permute-start.22) | collective-permute-done | bytes 262176 | tf_op jit(solution)/shard_map/ppermute | solution.py:118
  267.3 5.7 %collective-permute-done.23 = bf16[256,512]{1,0:T(8,128)(2,1)S(1)} collective-permute-done((bf16[256,512]{1,0:T(8,128)(2,1)S(1)}, bf16[256,512]{1,0:T(8,128)(2,1)S(1)}, u32[]{:S(2)}, u32[]{:S(2)}) %collective-permute-start.23) | collective-permute-done | bytes 262176 | tf_op jit(solution)/shard_map/ppermute | solution.py:118
  (134 shorter events, 27.9 us)
Async XLA Ops:
  6.5 34.2 %copy-start = (bf16[4,512,512]{2,1,0:T(8,128)(2,1)S(1)}, bf16[4,512,512]{2,1,0:T(8,128)(2,1)}, u32[]{:S(2)}) copy-start(bf16[4,512,512]{2,1,0:T(8,128)(2,1)} %param.19) | copy-start | bytes 6291460
  6.5 220.4 %all-gather.2.cloned.1.call-start = ((), (), s32[]{:S(2)}) async-start(), calls=%async_computation | async-start | bytes 1769472 | tf_op jit(solution)/shard_map/all_gather | solution.py:178
  7.9 1.2 copy-start.8
  11.6 4.8 %copy-start.5 = (bf16[256,2048]{1,0:T(8,128)(2,1)S(1)}, bf16[256,2048]{1,0:T(8,128)(2,1)}, u32[]{:S(2)}) copy-start(bf16[256,2048]{1,0:T(8,128)(2,1)} %param.22) | copy-start | bytes 3145732
  12.4 21.0 %collective-permute-start.2 = (bf16[2,256,512]{2,1,0:T(8,128)(2,1)}, bf16[2,256,512]{2,1,0:T(8,128)(2,1)}, u32[]{:S(2)}, u32[]{:S(2)}) collective-permute-start(bf16[2,256,512]{2,1,0:T(8,128)(2,1)} %pad_maximum_fusion.10), channel_id=1, source_target_pairs={{0,5},{1,4},{2,7},{3,6},{4,1},{5,0},{6,3},{7,2},{8,13},{9,12},{10,... | collective-permute-start | bytes 1572872 | tf_op jit(solution)/shard_map/ppermute | solution.py:118
  15.1 23.3 %collective-permute-start.1 = (bf16[2,256,512]{2,1,0:T(8,128)(2,1)}, bf16[2,256,512]{2,1,0:T(8,128)(2,1)}, u32[]{:S(2)}, u32[]{:S(2)}) collective-permute-start(bf16[2,256,512]{2,1,0:T(8,128)(2,1)} %pad_maximum_fusion.9), channel_id=1, source_target_pairs={{0,4},{1,5},{2,6},{3,7},{4,0},{5,1},{6,2},{7,3},{8,12},{9,13},{10,... | collective-permute-start | bytes 1572872 | tf_op jit(solution)/shard_map/ppermute | solution.py:118
  16.2 23.3 %collective-permute-start = (bf16[2,256,512]{2,1,0:T(8,128)(2,1)}, bf16[2,256,512]{2,1,0:T(8,128)(2,1)}, u32[]{:S(2)}, u32[]{:S(2)}) collective-permute-start(bf16[2,256,512]{2,1,0:T(8,128)(2,1)} %pad_maximum_fusion.8), channel_id=1, source_target_pairs={{0,1},{1,0},{2,3},{3,2},{4,5},{5,4},{6,7},{7,6},{8,9},{9,8},{10,11... | collective-permute-start | bytes 1572872 | tf_op jit(solution)/shard_map/ppermute | solution.py:118
  16.4 1.3 copy-start.9
  16.4 1.6 copy-start.10
  20.1 20.7 %collective-permute-start.3 = (bf16[3,256,512]{2,1,0:T(8,128)(2,1)}, bf16[3,256,512]{2,1,0:T(8,128)(2,1)}, u32[]{:S(2)}, u32[]{:S(2)}) collective-permute-start(bf16[3,256,512]{2,1,0:T(8,128)(2,1)} %pad_maximum_fusion.5), channel_id=1, source_target_pairs={{0,1},{1,0},{2,3},{3,2},{4,5},{5,4},{6,7},{7,6},{8,9},{9,8},{10,11... | collective-permute-start | bytes 2359304 | tf_op jit(solution)/shard_map/ppermute | solution.py:118
  21.4 19.4 %collective-permute-start.4 = (bf16[3,256,512]{2,1,0:T(8,128)(2,1)}, bf16[3,256,512]{2,1,0:T(8,128)(2,1)}, u32[]{:S(2)}, u32[]{:S(2)}) collective-permute-start(bf16[3,256,512]{2,1,0:T(8,128)(2,1)} %pad_maximum_fusion.6), channel_id=1, source_target_pairs={{0,2},{1,3},{2,0},{3,1},{4,6},{5,7},{6,4},{7,5},{8,10},{9,11},{10,... | collective-permute-start | bytes 2359304 | tf_op jit(solution)/shard_map/ppermute | solution.py:118
  22.9 3.2 %copy-start.11 = (bf16[1,256,512]{2,1,0:T(8,128)(2,1)S(1)}, bf16[1,256,512]{2,1,0:T(8,128)(2,1)}, u32[]{:S(2)}) copy-start(bf16[1,256,512]{2,1,0:T(8,128)(2,1)} %get-tuple-element.55) | copy-start | bytes 786436
  22.9 3.2 %copy-start.12 = (bf16[1,256,512]{2,1,0:T(8,128)(2,1)S(1)}, bf16[1,256,512]{2,1,0:T(8,128)(2,1)}, u32[]{:S(2)}) copy-start(bf16[1,256,512]{2,1,0:T(8,128)(2,1)} %get-tuple-element.88) | copy-start | bytes 786436
  24.2 2.9 %copy-start.22 = (s32[32]{0:T(128)S(1)}, s32[32]{0:T(128)}, u32[]{:S(2)}) copy-start(s32[32]{0:T(128)} %constant.160.clone) | copy-start | bytes 388
  24.2 9.1 %copy-start.20 = (s32[2]{0:T(128)S(1)}, s32[2]{0:T(128)}, u32[]{:S(2)}) copy-start(s32[2]{0:T(128)} %param.26) | copy-start | bytes 28
  24.2 9.1 %copy-start.21 = (s32[2]{0:T(128)S(1)}, s32[2]{0:T(128)}, u32[]{:S(2)}) copy-start(s32[2]{0:T(128)} %param.25) | copy-start | bytes 28
  27.1 13.5 %copy-start.14 = (bf16[256,512]{1,0:T(8,128)(2,1)S(1)}, bf16[256,512]{1,0:T(8,128)(2,1)}, u32[]{:S(2)}) copy-start(bf16[256,512]{1,0:T(8,128)(2,1)} %get-tuple-element.84) | copy-start | bytes 786436
  33.4 24.3 %collective-permute-start.5 = (bf16[3,256,512]{2,1,0:T(8,128)(2,1)S(1)}, bf16[3,256,512]{2,1,0:T(8,128)(2,1)S(1)}, u32[]{:S(2)}, u32[]{:S(2)}) collective-permute-start(bf16[3,256,512]{2,1,0:T(8,128)(2,1)S(1)} %pad_maximum_fusion.7), channel_id=1, source_target_pairs={{0,3},{1,2},{2,1},{3,0},{4,7},{5,6},{6,5},{7,4},{8,11},{9,10},{10,... | collective-permute-start | bytes 2359304 | tf_op jit(solution)/shard_map/ppermute | solution.py:118
  35.2 5.5 %copy-start.13 = (bf16[256,512]{1,0:T(8,128)(2,1)S(1)}, bf16[256,512]{1,0:T(8,128)(2,1)}, u32[]{:S(2)}) copy-start(bf16[256,512]{1,0:T(8,128)(2,1)} %get-tuple-element.59) | copy-start | bytes 786436
  60.3 1.7 copy-start.3
  60.3 3.0 %copy-start.19 = (f32[8,4096]{1,0:T(8,128)S(1)}, f32[8,4096]{1,0:T(8,128)}, u32[]{:S(2)}) copy-start(f32[8,4096]{1,0:T(8,128)} %param.27) | copy-start | bytes 393220
  62.0 10.7 %collective-permute-start.15 = (f32[192,512]{1,0:T(8,128)S(1)}, f32[192,512]{1,0:T(8,128)S(1)}, u32[]{:S(2)}, u32[]{:S(2)}) collective-permute-start(f32[192,512]{1,0:T(8,128)S(1)} %get-tuple-element.35), channel_id=1, source_target_pairs={{0,26},{2,0},{8,2},{10,8},{16,10},{18,16},{24,18},{26,24},{1,27},{... | collective-permute-start | bytes 1179656 | tf_op jit(solution)/shard_map/ppermute | solution.py:176
  63.1 18.9 %collective-permute-start.14 = (f32[192,512]{1,0:T(8,128)S(1)}, f32[192,512]{1,0:T(8,128)S(1)}, u32[]{:S(2)}, u32[]{:S(2)}) collective-permute-start(f32[192,512]{1,0:T(8,128)S(1)} %get-tuple-element.36), channel_id=1, source_target_pairs={{0,24},{2,26},{8,0},{10,2},{16,8},{18,10},{24,16},{26,18},{1,25},{... | collective-permute-start | bytes 1179656 | tf_op jit(solution)/shard_map/ppermute | solution.py:176
  63.3 58.8 %collective-permute-start.13 = (f32[192,512]{1,0:T(8,128)S(1)}, f32[192,512]{1,0:T(8,128)S(1)}, u32[]{:S(2)}, u32[]{:S(2)}) collective-permute-start(f32[192,512]{1,0:T(8,128)S(1)} %get-tuple-element.37), channel_id=1, source_target_pairs={{0,18},{2,24},{8,26},{10,0},{16,2},{18,8},{24,10},{26,16},{1,19},{... | collective-permute-start | bytes 1179656 | tf_op jit(solution)/shard_map/ppermute | solution.py:176
  66.7 63.9 %collective-permute-start.12 = (f32[192,512]{1,0:T(8,128)}, f32[192,512]{1,0:T(8,128)}, u32[]{:S(2)}, u32[]{:S(2)}) collective-permute-start(f32[192,512]{1,0:T(8,128)} %get-tuple-element.38), channel_id=1, source_target_pairs={{0,16},{2,18},{8,24},{10,26},{16,0},{18,2},{24,8},{26,10},{1,17},{... | collective-permute-start | bytes 1179656 | tf_op jit(solution)/shard_map/ppermute | solution.py:176
  66.7 64.8 %collective-permute-start.11 = (f32[192,512]{1,0:T(8,128)S(1)}, f32[192,512]{1,0:T(8,128)}, u32[]{:S(2)}, u32[]{:S(2)}) collective-permute-start(f32[192,512]{1,0:T(8,128)S(1)} %get-tuple-element.39), channel_id=1, source_target_pairs={{0,10},{2,16},{8,18},{10,24},{16,26},{18,0},{24,2},{26,8},{1,11},{... | collective-permute-start | bytes 1179656 | tf_op jit(solution)/shard_map/ppermute | solution.py:176
  72.7 14.6 %copy-start.15 = (f32[192,512]{1,0:T(8,128)}, f32[192,512]{1,0:T(8,128)S(1)}, u32[]{:S(2)}) copy-start(f32[192,512]{1,0:T(8,128)S(1)} %collective-permute-done.15) | copy-start | bytes 1179652
  72.7 62.4 %collective-permute-start.10 = (f32[192,512]{1,0:T(8,128)S(1)}, f32[192,512]{1,0:T(8,128)}, u32[]{:S(2)}, u32[]{:S(2)}) collective-permute-start(f32[192,512]{1,0:T(8,128)S(1)} %get-tuple-element.40), channel_id=1, source_target_pairs={{0,8},{2,10},{8,16},{10,18},{16,24},{18,26},{24,0},{26,2},{1,9},{3... | collective-permute-start | bytes 1179656 | tf_op jit(solution)/shard_map/ppermute | solution.py:176
  82.0 5.3 %copy-start.16 = (f32[192,512]{1,0:T(8,128)}, f32[192,512]{1,0:T(8,128)S(1)}, u32[]{:S(2)}) copy-start(f32[192,512]{1,0:T(8,128)S(1)} %collective-permute-done.14) | copy-start | bytes 1179652
  82.1 53.3 %collective-permute-start.9 = (f32[192,512]{1,0:T(8,128)S(1)}, f32[192,512]{1,0:T(8,128)}, u32[]{:S(2)}, u32[]{:S(2)}) collective-permute-start(f32[192,512]{1,0:T(8,128)S(1)} %get-tuple-element.34), channel_id=1, source_target_pairs={{0,2},{2,8},{8,10},{10,16},{16,18},{18,24},{24,26},{26,0},{1,3},{3... | collective-permute-start | bytes 1179656 | tf_op jit(solution)/shard_map/ppermute | solution.py:176
  122.0 0.7 copy-start.17
  122.8 76.1 %collective-permute-start.17 = (bf16[2,1024,512]{2,1,0:T(8,128)(2,1)}, bf16[2,1024,512]{2,1,0:T(8,128)(2,1)}, u32[]{:S(2)}, u32[]{:S(2)}) collective-permute-start(bf16[2,1024,512]{2,1,0:T(8,128)(2,1)} %slice.104), channel_id=1, source_target_pairs={{0,4},{1,5},{2,6},{3,7},{4,8},{5,9},{6,10},{7,11},{8,12},{9,13},{1... | collective-permute-start | bytes 6291464 | tf_op jit(solution)/shard_map/ppermute | solution.py:190
  130.6 10.5 %collective-permute-start.6 = (f32[1,260]{1,0:T(1,128)S(1)}, f32[1,260]{1,0:T(1,128)S(1)}, u32[]{:S(2)}, u32[]{:S(2)}) collective-permute-start(f32[1,260]{1,0:T(1,128)S(1)} %broadcast_in_dim.37), channel_id=1, source_target_pairs={{0,1},{1,0},{2,3},{3,2},{4,5},{5,4},{6,7},{7,6},{8,9},{9,8},{10,11... | collective-permute-start | bytes 3128 | tf_op jit(solution)/shard_map/ppermute | solution.py:118
  131.5 9.5 %collective-permute-start.7 = (f32[1,260]{1,0:T(1,128)S(1)}, f32[1,260]{1,0:T(1,128)S(1)}, u32[]{:S(2)}, u32[]{:S(2)}) collective-permute-start(f32[1,260]{1,0:T(1,128)S(1)} %broadcast_in_dim.37), channel_id=1, source_target_pairs={{0,2},{1,3},{2,0},{3,1},{4,6},{5,7},{6,4},{7,5},{8,10},{9,11},{10,... | collective-permute-start | bytes 3128 | tf_op jit(solution)/shard_map/ppermute | solution.py:118
  135.1 6.1 %collective-permute-start.8 = (f32[1,260]{1,0:T(1,128)S(1)}, f32[1,260]{1,0:T(1,128)S(1)}, u32[]{:S(2)}, u32[]{:S(2)}) collective-permute-start(f32[1,260]{1,0:T(1,128)S(1)} %broadcast_in_dim.37), channel_id=1, source_target_pairs={{0,3},{1,2},{2,1},{3,0},{4,7},{5,6},{6,5},{7,4},{8,11},{9,10},{10,... | collective-permute-start | bytes 3128 | tf_op jit(solution)/shard_map/ppermute | solution.py:118
  137.4 2.0 collective-permute-start.16
  139.4 0.7 copy-start.18
  227.0 14.1 %copy-start.2 = (bf16[1536,512]{1,0:T(8,128)(2,1)S(1)}, bf16[1536,512]{1,0:T(8,128)(2,1)}, u32[]{:S(2)}) copy-start(bf16[1536,512]{1,0:T(8,128)(2,1)} %all-gather.2.cloned.1.call-done) | copy-start | bytes 4718596
  230.6 8.3 %collective-permute-start.20 = (f32[8,128]{1,0:T(8,128)S(1)}, f32[8,128]{1,0:T(8,128)S(1)}, u32[]{:S(2)}, u32[]{:S(2)}) collective-permute-start(f32[8,128]{1,0:T(8,128)S(1)} %broadcast_in_dim.38), channel_id=1, source_target_pairs={{0,3},{1,2},{2,1},{3,0},{4,7},{5,6},{6,5},{7,4},{8,11},{9,10},{10,... | collective-permute-start | bytes 12296 | tf_op jit(solution)/shard_map/ppermute | solution.py:118
  236.8 2.5 collective-permute-start.19
  236.8 2.5 collective-permute-start.18
  244.9 1.2 copy-start.6
  252.9 3.1 %copy-start.4 = (f32[1024,512]{1,0:T(8,128)S(1)}, f32[1024,512]{1,0:T(8,128)}, u32[]{:S(2)}) copy-start(f32[1024,512]{1,0:T(8,128)} %pad_maximum_fusion.1) | copy-start | bytes 6291460
  257.9 15.9 %copy-start.1 = (bf16[4,512,512]{2,1,0:T(8,128)(2,1)S(1)}, bf16[4,512,512]{2,1,0:T(8,128)(2,1)}, u32[]{:S(2)}) copy-start(bf16[4,512,512]{2,1,0:T(8,128)(2,1)} %param.19) | copy-start | bytes 6291460
  258.1 2.9 %collective-permute-start.21 = (bf16[256,512]{1,0:T(8,128)(2,1)S(1)}, bf16[256,512]{1,0:T(8,128)(2,1)S(1)}, u32[]{:S(2)}, u32[]{:S(2)}) collective-permute-start(bf16[256,512]{1,0:T(8,128)(2,1)S(1)} %get-tuple-element.45), channel_id=1, source_target_pairs={{0,1},{1,0},{2,3},{3,2},{4,5},{5,4},{6,7},{7,6},{8,9},{9,8},{10,11... | collective-permute-start | bytes 786440 | tf_op jit(solution)/shard_map/ppermute | solution.py:118
  259.3 7.9 %collective-permute-start.22 = (bf16[256,512]{1,0:T(8,128)(2,1)S(1)}, bf16[256,512]{1,0:T(8,128)(2,1)S(1)}, u32[]{:S(2)}, u32[]{:S(2)}) collective-permute-start(bf16[256,512]{1,0:T(8,128)(2,1)S(1)} %get-tuple-element.44), channel_id=1, source_target_pairs={{0,2},{1,3},{2,0},{3,1},{4,6},{5,7},{6,4},{7,5},{8,10},{9,11},{10,... | collective-permute-start | bytes 786440 | tf_op jit(solution)/shard_map/ppermute | solution.py:118
  259.5 13.5 %collective-permute-start.23 = (bf16[256,512]{1,0:T(8,128)(2,1)S(1)}, bf16[256,512]{1,0:T(8,128)(2,1)S(1)}, u32[]{:S(2)}, u32[]{:S(2)}) collective-permute-start(bf16[256,512]{1,0:T(8,128)(2,1)S(1)} %get-tuple-element.43), channel_id=1, source_target_pairs={{0,3},{1,2},{2,1},{3,0},{4,7},{5,6},{6,5},{7,4},{8,11},{9,10},{10,... | collective-permute-start | bytes 786440 | tf_op jit(solution)/shard_map/ppermute | solution.py:118
  267.2 5.7 %copy-start.7 = (bf16[256,2048]{1,0:T(8,128)(2,1)}, bf16[256,2048]{1,0:T(8,128)(2,1)S(1)}, u32[]{:S(2)}) copy-start(bf16[256,2048]{1,0:T(8,128)(2,1)S(1)} %constant_dynamic-update-slice_fusion.1) | copy-start | bytes 3145732
Sparse Core Ops, SparseCore 0:
  140.3 57.0 all-gather.1
